TPU v7x, 128 devices: a whole 4x4x4 slice. The times are simulated.
128 devices in a mesh: lon: 8 (over y, z_hi), lat: 16 (over z_lo, x, core).
Axes of the slice: x: 4, y: 4, z: 4 (z_hi: 2, z_lo: 2; z = z_hi * 2 + z_lo), core: 2. Of those that a mesh axis runs over, the one named last changes fastest.
Arguments:
- grid_field: bfloat16 [192, 192, 3, 512], P('lon', 'lat'), may hold values from -6 to 6
- fine_weights: bfloat16 [512, 2048], replicated, may hold values from -0.25 to 0.25
- fine_gain: float32 [512], replicated, may hold values from 0.1 to 1.9
- fine_scales: float32 [8], replicated, may hold values from 4 to 16
- merge_gain: float32 [2048], replicated, may hold values from 0.1 to 1.9
- merge_weight: bfloat16 [2048, 1024], replicated, may hold values from -0.125 to 0.125
- coarse_weights: bfloat16 [1024, 4096], replicated, may hold values from -0.1875 to 0.1875
- coarse_gain: float32 [1024], replicated, may hold values from 0.1 to 1.9
- coarse_scales: float32 [16], replicated, may hold values from 4 to 16
- cot_fine: bfloat16 [192, 192, 3, 512], P('lon', 'lat'), may hold values from -6 to 6
- cot_coarse: bfloat16 [96, 96, 3, 1024], P('lon', 'lat'), may hold values from -6 to 6
Outputs:
- coarse_out: bfloat16 [96, 96, 3, 1024], P('lon', 'lat')
- grad_input: bfloat16 [192, 192, 3, 512], P('lon', 'lat')
- grad_fine_weights: float32 [512, 2048], P(('lon', 'lat'))
All inputs are finite; a program needn't handle non-finite values.
Results may differ from a plain program's by a relative error of at most 0.019.
Values may be sent and summed in bfloat16 or wider, within the bound.
No kernel may reach another device: no remote copies, remote signals or barrier semaphores. Data moves between devices by JAX's collectives and lax.ppermute only.
A program may use at most 192 MiB of HBM per device.

v0:
```python
import functools

import jax
import jax.numpy as jnp
from jax import lax
from jax.experimental import pallas as pl
from jax.experimental.pallas import tpu as pltpu
from jax.sharding import Mesh, PartitionSpec as P

LAT_AXES = ("chip", "core")
F32 = jnp.float32
BF16 = jnp.bfloat16
EPS_NORM = 1e-05
EPS_HEAD = 1e-06
D1, D2, H1, H2 = 512, 1024, 8, 16
HEAD = 64
TOK = 216
LON, LAT, LEV = 24, 12, 3
GROUPS = LAT * LEV
EDGE = 9
ROWS = GROUPS * LON
WIN = 12
FINE_BATCH, COARSE_BATCH, BACK_BATCH = 8, 4, 8
MIB = 1024 * 1024


def dot(left, right, left_dim, right_dim):
    return lax.dot_general(
        left, right, (((left_dim,), (right_dim,)), ((), ())), preferred_element_type=F32
    )


def mean_last(values):
    return jnp.mean(values, -1, keepdims=True)


def normalize(values):
    center = values - mean_last(values)
    inverse = lax.rsqrt(mean_last(center * center) + EPS_NORM)
    return center * inverse, inverse


def norm_back(scaled, normed, inverse):
    return inverse * (scaled - mean_last(scaled) - normed * mean_last(scaled * normed))


def keep_matrix(last_ref):
    half = TOK // 2
    keys = lax.broadcasted_iota(jnp.int32, (TOK, TOK), 0) >= half
    queries = lax.broadcasted_iota(jnp.int32, (TOK, TOK), 1) >= half
    apart = jnp.where(keys == queries, 0.0, 1.0)
    return 1.0 - apart * last_ref[0].astype(F32)


def unit_rows(values):
    inverse = lax.rsqrt(jnp.mean(values * values, 0, keepdims=True) + EPS_HEAD)
    return values * inverse, inverse


def softmax_rows(scores, keep):
    raw = jnp.exp(scores) * keep
    return raw * (1.0 / jnp.sum(raw, 0, keepdims=True))


def heads_back(grads, parts, softs, rounds, inverses, scales):
    grad_probs = [dot(part[2], grad, 0, 0) for part, grad in zip(parts, grads)]
    grad_values = [dot(grad, soft, 1, 1) for grad, soft in zip(grads, rounds)]
    grad_scores = [
        (soft * (probs - jnp.sum(probs * soft, 0, keepdims=True))).astype(BF16)
        for probs, soft in zip(grad_probs, softs)
    ]
    grad_q = [dot(part[1], scores, 1, 0) for part, scores in zip(parts, grad_scores)]
    grad_k = [dot(part[0], scores, 1, 1) for part, scores in zip(parts, grad_scores)]
    results = []
    for index, part in enumerate(parts):
        scale, (q_inverse, k_inverse) = scales[index], inverses[index]
        q_wide, k_wide = part[0].astype(F32), part[1].astype(F32)
        q_mean = jnp.mean(grad_q[index] * q_wide, 0, keepdims=True)
        k_mean = jnp.mean(grad_k[index] * k_wide, 0, keepdims=True)
        results.append((
            q_inverse * (grad_q[index] * scale - q_wide * (q_mean * (1.0 / scale))),
            k_inverse * (grad_k[index] - k_wide * k_mean),
            grad_values[index],
        ))
    return results


def head_rows(part, width, head):
    if isinstance(head, int):
        return slice(part * width + head * HEAD, part * width + head * HEAD + HEAD)
    return pl.ds(pl.multiple_of(part * width + head * HEAD, HEAD), HEAD)


def head_parts(head, width, scale, qkv):
    q_unit, q_inverse = unit_rows(qkv[head_rows(0, width, head), :])
    k_unit, k_inverse = unit_rows(qkv[head_rows(1, width, head), :])
    v_round = qkv[head_rows(2, width, head), :].astype(BF16)
    return (q_unit * scale).astype(BF16), k_unit.astype(BF16), v_round, q_inverse, k_inverse


def edges_kernel(x_ref, lat_ref, lon_ref, corner_ref, lon_rows, corner_rows):
    tile = x_ref[...].astype(F32).reshape(GROUPS, LON, D1)
    lat_ref[...] = tile[:EDGE].reshape(EDGE * LON, D1).astype(BF16)
    for group in range(GROUPS):
        rows = tile[group, 0:6]
        if group < EDGE:
            corner_rows[6 * group : 6 * group + 6, :] = rows
        else:
            lon_rows[6 * (group - EDGE) : 6 * (group - EDGE) + 6, :] = rows
    lon_ref[...] = lon_rows[...].astype(BF16)
    corner_ref[...] = corner_rows[...].astype(BF16)


def turn_kernel(w_ref, wt_ref):
    for part in range(3):
        cols = slice(part * D1, part * D1 + D1)
        wt_ref[cols, :] = w_ref[:, cols].T


def fine_forward_kernel(side, *refs):
    if side == 0:
        (x_ref, lat_ref, wt_ref, w_ref, gain_ref, scale_ref, last_ref,
         y_ref, ylat_ref, ylon_ref, ycor_ref, xw_ref, qkv_ref, inv_ref, soft_ref, att_ref,
         wins, qkv, keep, lon_rows, corner_rows) = refs
    else:
        (x_ref, lat_ref, lon_ref, corner_ref, first_ref, wt_ref, w_ref, gain_ref, scale_ref, last_ref,
         y_ref, ylat_ref, xw_ref, qkv_ref, inv_ref, soft_ref, att_ref, wins, qkv, keep) = refs
    tile = x_ref[...].astype(F32).reshape(GROUPS, LON, D1)
    lat_rows = lat_ref[...].astype(F32).reshape(EDGE, LON, D1)
    if side == 1:
        lon_in = lon_ref[...].astype(F32)
        corner_in = corner_ref[...].astype(F32)
    for group in range(GROUPS):
        source = tile[group + EDGE] if group + EDGE < GROUPS else lat_rows[group + EDGE - GROUPS]
        win, row = group // 18, WIN * (group % 18)
        if side == 0:
            wins[win, row : row + WIN, :] = source[6:18]
        else:
            wins[win, row : row + 6, :] = source[18:24]
            if group + EDGE < GROUPS:
                halo = lon_in[6 * group : 6 * group + 6]
            else:
                halo = corner_in[6 * (group + EDGE - GROUPS) : 6 * (group + EDGE - GROUPS) + 6]
            wins[win, row + 6 : row + WIN, :] = halo
    keep[...] = keep_matrix(last_ref)

    def window(win, carry):
        values = wins[win]
        xw_ref[win] = values.astype(BF16)
        normed = (normalize(values)[0] * gain_ref[...]).astype(BF16)
        for part in range(3):
            qkv[part * D1 : part * D1 + D1, :] = dot(
                wt_ref[part * D1 : part * D1 + D1, :], normed, 1, 1
            )
        use_keep = jnp.where(win >= 1, keep[...], 1.0)
        for start in range(0, H1, FINE_BATCH):
            batch = range(start, start + FINE_BATCH)
            parts = []
            for head in batch:
                q_scaled, k_round, v_round, q_inverse, k_inverse = head_parts(
                    head, D1, scale_ref[head] / HEAD, qkv
                )
                qkv_ref[win, head_rows(0, D1, head), :] = q_scaled
                qkv_ref[win, head_rows(1, D1, head), :] = k_round
                qkv_ref[win, head_rows(2, D1, head), :] = v_round
                inv_ref[win, head : head + 1, :] = q_inverse
                inv_ref[win, H1 + head : H1 + head + 1, :] = k_inverse
                parts.append((q_scaled, k_round, v_round))
            scores = [dot(k_round, q_scaled, 0, 0) for q_scaled, k_round, _ in parts]
            softs = [softmax_rows(score, use_keep).astype(BF16) for score in scores]
            for head, soft, part in zip(batch, softs, parts):
                soft_ref[win, head] = soft
                att_ref[win, head_rows(0, D1, head), :] = dot(part[2], soft, 1, 0).astype(BF16)
        result = values + dot(att_ref[win], w_ref[:, 3 * D1 :], 0, 0)
        wins[win] = result
        y_ref[win] = result.astype(BF16)
        return carry

    lax.fori_loop(0, 2, window, 0)
    if side == 0:
        ylat_ref[...] = wins[0, 0:112, :].astype(BF16)
        for group in range(GROUPS):
            rows = wins[group // 18, WIN * (group % 18) : WIN * (group % 18) + 6, :]
            if group < EDGE:
                corner_rows[6 * group : 6 * group + 6, :] = rows
            else:
                lon_rows[6 * (group - EDGE) : 6 * (group - EDGE) + 6, :] = rows
        ylon_ref[...] = lon_rows[...].astype(BF16)
        ycor_ref[...] = corner_rows[...].astype(BF16)
    else:
        ylat_ref[0:112, :] = first_ref[...]
        ylat_ref[112:224, :] = wins[0, 0:112, :].astype(BF16)


def coarse_kernel(
    y0_ref, y1_ref, lat_ref, lon_ref, corner_ref, cotc_ref, mgain_ref, mw_ref, cw_ref, gain_ref,
    scale_ref, last_ref,
    att, val_ref, g_ref, glat_ref, glon_ref, gcor_ref,
    near, far, halo, cells, merged, mnorm, minv, qkv, gqkv, gatt, turned, keep, lon_rows, corner_rows, cot_rows,
):
    for group in range(18):
        cot_rows[WIN * group : WIN * group + WIN, :] = cotc_ref[group].astype(F32)
    cot = cot_rows[...].astype(BF16)
    for cut in range(4):
        lanes = slice(cut * 128, cut * 128 + 128)
        for win in range(2):
            near[cut, TOK * win : TOK * win + TOK, :] = y0_ref[win, :, lanes].astype(F32)
            far[cut, TOK * win : TOK * win + TOK, :] = y1_ref[win, :, lanes].astype(F32)
        near[cut, 2 * TOK :, :] = lat_ref[0:112, lanes].astype(F32)
        far[cut, 2 * TOK :, :] = lat_ref[112:224, lanes].astype(F32)
        halo[cut, 0:162, :] = lon_ref[:, lanes].astype(F32)
        halo[cut, 162:TOK, :] = corner_ref[:, lanes].astype(F32)
    for group in range(18):
        for part in range(4):
            cell = (2 * (group // LEV) + part % 2) * LEV + group % LEV
            source, odd, row = WIN * (cell + EDGE), part // 2, WIN * group
            for cut in range(4):
                lanes = slice(part * D1 + cut * 128, part * D1 + cut * 128 + 128)
                merged[row : row + 3, lanes] = near[cut, pl.ds(source + 6 + odd, 3, stride=2), :]
                merged[row + 3 : row + 9, lanes] = far[cut, pl.ds(source + odd, 6, stride=2), :]
                merged[row + 9 : row + WIN, lanes] = halo[cut, pl.ds(6 * cell + odd, 3, stride=2), :]
    for start in range(0, TOK, 72):
        normed, inverse = normalize(merged[start : start + 72, :])
        merged[start : start + 72, :] = normed
        minv[start : start + 72, :] = jnp.broadcast_to(inverse, (72, 128))
        mnorm[start : start + 72, :] = normed * mgain_ref[...]
    keep[...] = keep_matrix(last_ref)
    values = dot(mnorm[...].astype(BF16), mw_ref[...], 1, 0).astype(BF16).astype(F32)
    value_norm, value_inverse = normalize(values)
    normed = (value_norm * gain_ref[...]).astype(BF16)
    for start in range(0, 3 * D2, 512):
        qkv[start : start + 512, :] = dot(normed, cw_ref[:, start : start + 512], 1, 0).T
    for start in range(0, D2, 512):
        gatt[start : start + 512, :] = dot(
            cw_ref[start : start + 512, 3 * D2 :], cot, 1, 1
        ).astype(BF16)

    def heads(step, carry):
        batch = [step * COARSE_BATCH + inner for inner in range(COARSE_BATCH)]
        scales = [scale_ref[head] / HEAD for head in batch]
        parts = [head_parts(head, D2, scale, qkv) for head, scale in zip(batch, scales)]
        scores = [dot(part[1], part[0], 0, 0) for part in parts]
        softs = [softmax_rows(score, keep[...]) for score in scores]
        rounds = [soft.astype(BF16) for soft in softs]
        for head, soft, part in zip(batch, rounds, parts):
            att[head_rows(0, D2, head), :] = dot(part[2], soft, 1, 0).astype(BF16)
        grads = [gatt[head_rows(0, D2, head), :] for head in batch]
        results = heads_back(grads, parts, softs, rounds, [part[3:] for part in parts], scales)
        for head, result in zip(batch, results):
            for part in range(3):
                gqkv[head_rows(part, D2, head), :] = result[part].astype(BF16)
        return carry

    lax.fori_loop(0, H2 // COARSE_BATCH, heads, 0)
    val_ref[...] = values.astype(BF16)
    for start in range(0, D2, 256):
        turned[start : start + 256, :] = dot(
            cw_ref[start : start + 256, : 3 * D2], gqkv[...], 1, 0
        )
    scaled = turned[...].T * gain_ref[...]
    grad_in = cot_rows[...] + norm_back(scaled, value_norm, value_inverse)
    grad_in = grad_in.astype(BF16)
    for part in range(4):
        cols = slice(part * D1, part * D1 + D1)
        mnorm[:, cols] = dot(grad_in, mw_ref[cols, :], 1, 1) * mgain_ref[:, cols]
    for start in range(0, TOK, 72):
        mnorm[start : start + 72, :] = norm_back(
            mnorm[start : start + 72, :], merged[start : start + 72, :], minv[start : start + 72, 0:1]
        )
    for group in range(18):
        for part in range(4):
            target = (2 * (group // LEV) + part % 2) * LEV + group % LEV
            for cut in range(4):
                cells[cut, target, pl.ds(part // 2, WIN, stride=2), :] = mnorm[
                    WIN * group : WIN * group + WIN,
                    part * D1 + cut * 128 : part * D1 + cut * 128 + 128,
                ]
    done = jnp.concatenate([cells[cut] for cut in range(4)], -1)
    g_ref[...] = done.reshape(ROWS, D1).astype(BF16)
    glat_ref[...] = done[GROUPS - EDGE :].reshape(EDGE * LON, D1).astype(BF16)
    for group in range(GROUPS):
        rows = done[group, 18:24]
        if group < GROUPS - EDGE:
            lon_rows[6 * group : 6 * group + 6, :] = rows
        else:
            at = 6 * (group + EDGE - GROUPS)
            corner_rows[at : at + 6, :] = rows
    glon_ref[...] = lon_rows[...].astype(BF16)
    gcor_ref[...] = corner_rows[...].astype(BF16)


def coarse_out_kernel(att_ref, val_ref, cw_ref, out_ref):
    result = val_ref[...].astype(F32) + dot(att_ref[...], cw_ref[:, 3 * D2 :], 0, 0)
    for group in range(18):
        out_ref[group] = result[WIN * group : WIN * group + WIN].astype(BF16)


def normed_kernel(xw0_ref, xw1_ref, gain_ref, normt0_ref, normt1_ref):
    for xw_ref, normt_ref in ((xw0_ref, normt0_ref), (xw1_ref, normt1_ref)):
        normt_ref[...] = jnp.zeros_like(normt_ref)
        for win in range(2):
            normed = (normalize(xw_ref[win].astype(F32))[0] * gain_ref[...]).astype(BF16)
            normt_ref[win, :, 0:TOK] = normed.T


def fine_backward_kernel(side, *refs):
    if side == 1:
        (g_ref, lat_ref, cot_ref, clat_ref, clon_ref, ccor_ref,
         qkv_ref, inv_ref, soft_ref, att_ref, w_ref, scale_ref, gq_ref, e_ref, wins, gatt) = refs
        lon_cot = clon_ref[...].astype(F32)
        corner_cot = ccor_ref[...].astype(F32)
    else:
        (g_ref, lat_ref, lon_ref, corner_ref, cot_ref, clat_ref, qkv_ref, inv_ref, soft_ref, att_ref, w_ref,
         scale_ref, core_ref, gq1_ref, e1_ref, att1_ref, normt_ref, normt1_ref,
         gq_ref, e_ref, keep_ref, send_ref, wins, gatt) = refs
        lon_in = lon_ref[...].astype(F32)
        corner_in = corner_ref[...].astype(F32)
    tile = g_ref[...].astype(F32).reshape(GROUPS, LON, D1)
    lat_rows = lat_ref[...].astype(F32).reshape(EDGE, LON, D1)
    cot_tile = cot_ref[...].astype(F32).reshape(GROUPS, LON, D1)
    cot_lat = clat_ref[...].astype(F32).reshape(EDGE, LON, D1)
    for group in range(GROUPS):
        source = lat_rows[group] if group < EDGE else tile[group - EDGE]
        win, row = group // 18, WIN * (group % 18)
        inside = group + EDGE < GROUPS
        cot = cot_tile[group + EDGE] if inside else cot_lat[group + EDGE - GROUPS]
        if side == 1:
            at = 6 * group if inside else 6 * (group + EDGE - GROUPS)
            halo = lon_cot[at : at + 6] if inside else corner_cot[at : at + 6]
            wins[win, row : row + 6, :] = source[6:12] + cot[18:24]
            wins[win, row + 6 : row + WIN, :] = source[12:18] + halo
        else:
            if group < EDGE:
                halo = corner_in[6 * group : 6 * group + 6]
            else:
                halo = lon_in[6 * (group - EDGE) : 6 * (group - EDGE) + 6]
            wins[win, row : row + 6, :] = halo + cot[6:12]
            wins[win, row + 6 : row + WIN, :] = source[0:6] + cot[12:18]
    gq_ref[...] = jnp.zeros_like(gq_ref)

    def window(win, carry):
        cot = wins[win].astype(BF16)
        e_ref[win] = cot
        gatt[...] = dot(w_ref[:, 3 * D1 :], cot, 1, 1).astype(BF16)
        for start in range(0, H1, BACK_BATCH):
            batch = range(start, start + BACK_BATCH)
            rounds = [soft_ref[win, head] for head in batch]
            results = heads_back(
                [gatt[head_rows(0, D1, head), :] for head in batch],
                [[qkv_ref[win, head_rows(part, D1, head), :] for part in range(3)] for head in batch],
                [soft.astype(F32) for soft in rounds],
                rounds,
                [(inv_ref[win, head : head + 1, :], inv_ref[win, H1 + head : H1 + head + 1, :]) for head in batch],
                [scale_ref[head] / HEAD for head in batch],
            )
            for head, result in zip(batch, results):
                for part in range(3):
                    gq_ref[win, head_rows(part, D1, head), 0:TOK] = result[part].astype(BF16)
        return carry

    lax.fori_loop(0, 2, window, 0)
    if side == 0:
        sums = []
        for part in range(3):
            cols = slice(part * D1, part * D1 + D1)
            total = dot(normt_ref[0], gq_ref[0, cols, :], 1, 1) + dot(normt_ref[1], gq_ref[1, cols, :], 1, 1)
            total += dot(normt1_ref[0], gq1_ref[0, cols, :], 1, 1)
            sums.append(total + dot(normt1_ref[1], gq1_ref[1, cols, :], 1, 1))
        total = dot(att_ref[0], e_ref[0], 1, 0) + dot(att_ref[1], e_ref[1], 1, 0)
        sums.append(total + dot(att1_ref[0], e1_ref[0], 1, 0) + dot(att1_ref[1], e1_ref[1], 1, 0))
        for part in range(2):
            cols = slice(part * D1, part * D1 + D1)
            first = core_ref[0] == 0
            keep_ref[:, cols] = jnp.where(first, sums[part], sums[2 + part]).astype(BF16)
            send_ref[:, cols] = jnp.where(first, sums[2 + part], sums[part]).astype(BF16)


def fine_input_kernel(
    gq0_ref, gq1_ref, e0_ref, e1_ref, xw0_ref, xw1_ref, w_ref, gain_ref,
    g0_ref, g1_ref, glat_ref, glon_ref, gcor_ref, lat_rows, lon_rows, corner_rows,
):
    for side, (gq_ref, e_ref, xw_ref, g_ref) in enumerate(
        ((gq0_ref, e0_ref, xw0_ref, g0_ref), (gq1_ref, e1_ref, xw1_ref, g1_ref))
    ):
        for win in range(2):
            turned = dot(w_ref[:, : 3 * D1], gq_ref[win], 1, 0)
            scaled = turned.T[:TOK] * gain_ref[...]
            normed, inverse = normalize(xw_ref[win].astype(F32))
            grad_in = e_ref[win].astype(F32) + norm_back(scaled, normed, inverse)
            g_ref[win] = grad_in.astype(BF16)
            if win == 1:
                lat_rows[108 * side : 108 * side + 108, :] = grad_in[108:TOK]
            if side == 1:
                for group in range(18):
                    rows = grad_in[WIN * group + 6 : WIN * group + WIN]
                    at = 6 * (group + 18 * win)
                    if at < 162:
                        lon_rows[at : at + 6, :] = rows
                    else:
                        corner_rows[at - 162 : at - 156, :] = rows
    glat_ref[...] = lat_rows[...].astype(BF16)
    glon_ref[...] = lon_rows[...].astype(BF16)
    gcor_ref[...] = corner_rows[...].astype(BF16)


def assemble_kernel(g0_ref, g1_ref, lat_ref, lon_ref, corner_ref, out_ref, full):
    first = [g0_ref[win].astype(F32) for win in range(2)]
    second = [g1_ref[win].astype(F32) for win in range(2)]
    lat_rows = lat_ref[...].astype(F32)
    lon_rows = lon_ref[...].astype(F32)
    corner_rows = corner_ref[...].astype(F32)
    for group in range(GROUPS):
        if group < EDGE:
            full[group, 0:6, :] = corner_rows[6 * group : 6 * group + 6]
            full[group, 6:18, :] = lat_rows[WIN * group : WIN * group + WIN]
            full[group, 18:24, :] = lat_rows[108 + WIN * group : 108 + WIN * group + 6]
        else:
            own = group - EDGE
            win, row = own // 18, WIN * (own % 18)
            full[group, 0:6, :] = lon_rows[6 * own : 6 * own + 6]
            full[group, 6:18, :] = first[win][row : row + WIN]
            full[group, 18:24, :] = second[win][row : row + 6]
    out_ref[...] = full[...].reshape(ROWS, D1).astype(BF16)


def call(kernel, outs, scratch, smem_from, args, name, flops, vmem):
    whole = pl.BlockSpec(memory_space=pltpu.VMEM)
    scalars = pl.BlockSpec(memory_space=pltpu.SMEM)
    return pl.pallas_call(
        kernel,
        out_shape=[jax.ShapeDtypeStruct(shape, kind) for shape, kind in outs],
        in_specs=[scalars if position in smem_from else whole for position in range(len(args))],
        out_specs=[whole] * len(outs),
        scratch_shapes=[pltpu.VMEM(shape, kind) for shape, kind in scratch],
        compiler_params=pltpu.CompilerParams(vmem_limit_bytes=vmem * MIB),
        cost_estimate=pl.CostEstimate(flops=flops, bytes_accessed=1 << 22, transcendentals=0),
        name=name,
    )(*args)


HALF = ((2, TOK, D1), BF16)
LAT_BLOCK = ((EDGE * LON, D1), BF16)
LON_BLOCK = ((162, D1), BF16)
CORNER = ((54, D1), BF16)
LON_ROWS = ((162, D1), F32)
CORNER_ROWS = ((54, D1), F32)


def edges(tile):
    return call(edges_kernel, [LAT_BLOCK, LON_BLOCK, CORNER], [LON_ROWS, CORNER_ROWS], (), (tile,), "edges", 2 * 10**9, 6)


def turn(weights):
    return call(turn_kernel, [((3 * D1, D1), BF16)], [], (), (weights,), "turn", 10**9, 6)[0]


def fine_forward(side, ins, weights, scalars):
    outs = [HALF] + ([((112, D1), BF16), LON_BLOCK, CORNER] if side == 0 else [((224, D1), BF16)])
    outs += [
        HALF,
        ((2, 3 * D1, TOK), BF16),
        ((2, 2 * H1, TOK), F32),
        ((2, H1, TOK, TOK), BF16),
        ((2, D1, TOK), BF16),
    ]
    scratch = [((2, TOK, D1), F32), ((3 * D1, TOK), F32), ((TOK, TOK), F32)]
    if side == 0:
        scratch += [LON_ROWS, CORNER_ROWS]
    args = (*ins, *weights, *scalars)
    smem = (len(args) - 2, len(args) - 1)
    kernel = functools.partial(fine_forward_kernel, side)
    out = call(kernel, outs, scratch, smem, args, "fine_forward_" + str(side), 10**10, 10)
    return out[:-5], out[-5:]


def coarse_both(ins, cot_coarse, mgain, mw, cw, gain, scales, last):
    outs = [((D2, TOK), BF16), ((TOK, D2), BF16), ((ROWS, D1), BF16), LAT_BLOCK, LON_BLOCK, CORNER]
    scratch = [
        ((4, 2 * TOK + 112, 128), F32),
        ((4, 2 * TOK + 112, 128), F32),
        ((4, TOK, 128), F32),
        ((4, GROUPS, LON, 128), F32),
        ((TOK, 4 * D1), F32),
        ((TOK, 4 * D1), F32),
        ((TOK, 128), F32),
        ((3 * D2, TOK), F32),
        ((3 * D2, TOK), BF16),
        ((D2, TOK), BF16),
        ((D2, TOK), F32),
        ((TOK, TOK), F32),
        LON_ROWS,
        CORNER_ROWS,
        ((TOK, D2), F32),
    ]
    args = (*ins, cot_coarse, mgain, mw, cw, gain, scales, last)
    return call(coarse_kernel, outs, scratch, (10, 11), args, "coarse_both", 2 * 10**10, 22)


def coarse_result(att, values, weights):
    return call(
        coarse_out_kernel, [((18, WIN, D2), BF16)], [], (), (att, values, weights), "coarse_out", 10**9, 16
    )[0]


def normed_turned(xw0, xw1, gain):
    outs = [((2, D1, 256), BF16)] * 2
    return call(normed_kernel, outs, [], (), (xw0, xw1, gain), "normed", 10**9, 8)


def fine_backward(side, ins, saved, weights, scales, core=(), other=()):
    outs = [((2, 3 * D1, 256), BF16), HALF]
    scratch = [((2, TOK, D1), F32), ((D1, TOK), BF16)]
    if side == 0:
        outs += [((D1, 2 * D1), BF16)] * 2
    args = (*ins, *saved, weights, scales, *core, *other)
    scalars = len(args) - len(other) - len(core) - 1
    smem = tuple(range(scalars, scalars + 1 + len(core)))
    kernel = functools.partial(fine_backward_kernel, side)
    return call(kernel, outs, scratch, smem, args, "fine_backward_" + str(side), 10**10, 14)


def fine_input(args):
    outs = [HALF, HALF, LAT_BLOCK, LON_BLOCK, CORNER]
    scratch = [((EDGE * LON, D1), F32), LON_ROWS, CORNER_ROWS]
    return call(fine_input_kernel, outs, scratch, (), args, "fine_input", 6 * 10**9, 8)


def assemble(args):
    scratch = [((GROUPS, LON, D1), F32)]
    return call(assemble_kernel, [((ROWS, D1), BF16)], scratch, (), args, "assemble", 2 * 10**9, 6)[0]


def ring(axis_size, step):
    return [(i, (i + step) % axis_size) for i in range(axis_size)]


def moved(block, axis, step):
    return lax.ppermute(block, axis, ring(lax.axis_size(axis), step))


def moved_both(block, step):
    nlon, nlat = lax.axis_size("lon"), lax.axis_size(LAT_AXES)
    route = [
        (i * nlat + j, ((i + step) % nlon) * nlat + (j + step) % nlat)
        for i in range(nlon)
        for j in range(nlat)
    ]
    return lax.ppermute(block, ("lon", *LAT_AXES), route)


def half_moved(tile, axis, dim, step):
    near, far = jnp.split(tile, 2, dim)
    if step < 0:
        return jnp.concatenate([far, moved(near, axis, step)], dim)
    return jnp.concatenate([moved(far, axis, step), near], dim)


def after(value, *others):
    return lax.optimization_barrier((value, *others))[0]


def chip_sum(part):
    pieces = lax.all_to_all(part.reshape(64, 8, 2 * D1), ("lon", "chip"), 0, 0)
    return jnp.sum(pieces.astype(F32), 0)


def own_rows(total, core):
    first = core == 0
    mine = jnp.where(first, total[:4], total[4:])
    other = lax.ppermute(jnp.where(first, total[4:], total[:4]), "core", [(0, 1), (1, 0)])
    return jnp.concatenate([jnp.where(first, mine, other), jnp.where(first, other, mine)], 1)


def on_device(
    grid_field, fine_weights, fine_gain, fine_scales, merge_gain, merge_weight, coarse_weights, coarse_gain,
    coarse_scales, cot_fine, cot_coarse,
):
    core = lax.axis_index("core").astype(jnp.int32).reshape(1)
    last = (lax.axis_index(LAT_AXES) == lax.axis_size(LAT_AXES) - 1).astype(jnp.int32).reshape(1)
    fine_gain = fine_gain.reshape(1, -1)
    tile = grid_field.transpose(1, 2, 0, 3).reshape(ROWS, D1)
    lat, lon, corner = edges(tile)
    lat, lon, corner = moved(lat, LAT_AXES, -1), moved(lon, "lon", -1), moved_both(corner, -1)
    cot_coarse = after(cot_coarse, lat).transpose(1, 2, 0, 3)
    cot_coarse = half_moved(cot_coarse, "lon", 2, -1)
    weights = (turn(fine_weights), fine_weights, fine_gain)
    scalars = (fine_scales, last)
    (y0, ylat, ylon, ycor), saved0 = fine_forward(0, (tile, lat), weights, scalars)
    ylon, ycor = moved(ylon, "lon", -1), moved_both(ycor, -1)
    cot_coarse = half_moved(after(cot_coarse, y0), LAT_AXES, 0, -1).reshape(18, WIN, D2)
    (y1, ylat), saved1 = fine_forward(1, (tile, lat, lon, corner, ylat), weights, scalars)
    ylat, ylon, ycor, cot_coarse = lax.optimization_barrier((ylat, ylon, ycor, cot_coarse))
    ylat = moved(ylat, LAT_AXES, -1)
    cot_tile = after(cot_fine, y1).transpose(1, 2, 0, 3).reshape(ROWS, D1)
    cot_edges = edges(cot_tile)
    cot_edges = (moved(cot_edges[0], LAT_AXES, -1), moved(cot_edges[1], "lon", -1), moved_both(cot_edges[2], -1))
    att, values, grad, glat, glon, gcor = coarse_both(
        (y0, y1, ylat, ylon, ycor), cot_coarse, merge_gain.reshape(1, -1), merge_weight,
        coarse_weights, coarse_gain.reshape(1, -1), coarse_scales, last,
    )
    (glat, glon, gcor), cot_edges = lax.optimization_barrier(((glat, glon, gcor), cot_edges))
    glat, glon, gcor = moved(glat, LAT_AXES, 1), moved(glon, "lon", 1), moved_both(gcor, 1)
    coarse_out = coarse_result(att, values, coarse_weights)
    normt0, normt1 = normed_turned(saved0[0], saved1[0], after(fine_gain, att))
    coarse_out, glat, normt0, normt1 = lax.optimization_barrier((coarse_out, glat, normt0, normt1))
    coarse_out = half_moved(coarse_out.reshape(LAT // 2, LEV, LON // 2, D2), "lon", 2, 1)
    gq1, e1 = fine_backward(1, (grad, glat, cot_tile, *cot_edges), saved1[1:], fine_weights, fine_scales)
    own, other = jnp.split(coarse_out, 2, 0)
    other = moved(other, LAT_AXES, 1)
    gq0, e0, keep, send = fine_backward(
        0, (grad, glat, glon, gcor, cot_tile, cot_edges[0]), saved0[1:], fine_weights, fine_scales,
        (core,), (gq1, e1, saved1[4], normt0, normt1),
    )
    sent = lax.ppermute(send, "core", [(0, 1), (1, 0)])
    g0, g1, lat, lon, corner = fine_input(
        (gq0, gq1, e0, e1, saved0[0], saved1[0], fine_weights, fine_gain)
    )
    lat, lon, corner = moved(lat, LAT_AXES, 1), moved(lon, "lon", 1), moved_both(corner, 1)
    sent, keep, g0 = lax.optimization_barrier((sent, keep, g0))
    part = (keep.astype(F32) + sent.astype(F32)).astype(BF16)
    total = chip_sum(part)
    share = own_rows(total, core[0])
    lat, lon, corner, other = (after(block, total) for block in (lat, lon, corner, other))
    grad_input = assemble((g0, g1, lat, lon, corner)).reshape(LAT, LEV, LON, D1)
    coarse_out = jnp.concatenate([other, own], 0)
    return coarse_out.transpose(2, 0, 1, 3), grad_input.transpose(2, 0, 1, 3), share


def solution(mesh):
    split = Mesh(mesh.devices.reshape(mesh.devices.shape[0], -1, 2), ("lon", *LAT_AXES))
    tile = P("lon", LAT_AXES, None, None)
    in_specs = (tile,) + (P(),) * 8 + (tile, tile)
    out_specs = (tile, tile, P(("lon", *LAT_AXES), None))
    return jax.shard_map(
        on_device, mesh=split, in_specs=in_specs, out_specs=out_specs, check_vma=False
    )
```

profile of v0, /device:TPU:1, one launch (start us, length us, event | category | flops | bytes accessed | tf_op | source)
XLA Modules:
  0.0 131.6 jit_solution(6082384552385500490)
XLA Ops:
  0.6 0.0 copy-start.2
  0.6 1.2 copy-done.2
  1.8 0.1 edges.2
  1.9 1.5 %collective-permute-start = (bf16[216,512]{1,0:T(8,128)(2,1)S(1)}, bf16[216,512]{1,0:T(8,128)(2,1)S(1)}, u32[]{:S(2)}, u32[]{:S(2)}) collective-permute-start(bf16[216,512]{1,0:T(8,128)(2,1)S(1)} %get-tuple-element.69), channel_id=1, source_target_pairs={{0,15},{1,0},{2,1},{3,2},{4,3},{5,4},{6,5},{7,6},{8,7},{9,8},{10,9... | collective-permute-start | bytes 663560 | tf_op jit(solution)/shard_map/ppermute | solution.py:538
  3.4 6.1 %collective-permute-start.1 = (bf16[162,512]{1,0:T(8,128)(2,1)S(1)}, bf16[162,512]{1,0:T(8,128)(2,1)S(1)}, u32[]{:S(2)}, u32[]{:S(2)}) collective-permute-start(bf16[162,512]{1,0:T(8,128)(2,1)S(1)} %get-tuple-element.71), channel_id=1, source_target_pairs={{0,112},{16,0},{32,16},{48,32},{64,48},{80,64},{96,80},{112,96},{1... | collective-permute-start | bytes 497672 | tf_op jit(solution)/shard_map/ppermute | solution.py:538
  9.5 3.2 %collective-permute-start.2 = (bf16[54,512]{1,0:T(8,128)(2,1)S(1)}, bf16[54,512]{1,0:T(8,128)(2,1)S(1)}, u32[]{:S(2)}, u32[]{:S(2)}) collective-permute-start(bf16[54,512]{1,0:T(8,128)(2,1)S(1)} %get-tuple-element.72), channel_id=1, source_target_pairs={{0,127},{1,112},{2,113},{3,114},{4,115},{5,116},{6,117},{7,118},{8... | collective-permute-start | bytes 165896 | tf_op jit(solution)/shard_map/ppermute | solution.py:548
  12.7 0.0 copy-start.9
  12.7 0.5 turn.1.refs_2_.refs_5_
  13.2 0.6 copy-done.14
  13.8 0.2 fusion.4
  14.0 3.5 %collective-permute-start.5 = (bf16[6,3,6,1024]{3,1,0,2:T(4,128)(2,1)S(1)}, bf16[6,3,6,1024]{3,1,0,2:T(4,128)(2,1)S(1)}, u32[]{:S(2)}, u32[]{:S(2)}) collective-permute-start(bf16[6,3,6,1024]{3,1,0,2:T(4,128)(2,1)S(1)} %get-tuple-element.142), channel_id=1, source_target_pairs={{0,112},{16,0},{32,16},{48,32},{64,48},{80,64},{96,80},{112,96},{1... | collective-permute-start | bytes 663560 | tf_op jit(solution)/shard_map/ppermute | solution.py:538
  17.5 4.4 %fine_forward_0.1 = (bf16[2,216,512]{2,1,0:T(8,128)(2,1)S(1)}, bf16[112,512]{1,0:T(8,128)(2,1)S(1)}, bf16[162,512]{1,0:T(8,128)(2,1)S(1)}, bf16[54,512]{1,0:T(8,...) custom-call(bf16[864,512]{1,0:T(8,128)(2,1)S(1)} %bitcast.26, ...), custom_call_target="tpu_custom_call" | custom-call | flops 10000000000 | bytes 4194304 | tf_op jit(solution)/shard_map/fine_forward_0/pallas_call | solution.py:429
  21.9 0.1 collective-permute-start.3
  22.0 2.7 %collective-permute-start.4 = (bf16[54,512]{1,0:T(8,128)(2,1)S(1)}, bf16[54,512]{1,0:T(8,128)(2,1)S(1)}, u32[]{:S(2)}, u32[]{:S(2)}) collective-permute-start(bf16[54,512]{1,0:T(8,128)(2,1)S(1)} %get-tuple-element.77), channel_id=1, source_target_pairs={{0,127},{1,112},{2,113},{3,114},{4,115},{5,116},{6,117},{7,118},{8... | collective-permute-start | bytes 165896 | tf_op jit(solution)/shard_map/ppermute | solution.py:548
  24.7 0.4 pad_maximum_fusion
  25.1 0.0 slice-start
  25.1 0.2 fusion.3
  25.3 2.8 %collective-permute-start.6 = (bf16[3,3,12,1024]{3,1,0,2:T(4,128)(2,1)S(1)}, bf16[3,3,12,1024]{3,1,0,2:T(4,128)(2,1)S(1)}, u32[]{:S(2)}, u32[]{:S(2)}) collective-permute-start(bf16[3,3,12,1024]{3,1,0,2:T(4,128)(2,1)S(1)} %get-tuple-element.140), channel_id=1, source_target_pairs={{0,15},{1,0},{2,1},{3,2},{4,3},{5,4},{6,5},{7,6},{8,7},{9,8},{10,9... | collective-permute-start | bytes 663560 | tf_op jit(solution)/shard_map/ppermute | solution.py:538
  28.1 4.3 %fine_forward_1.1 = (bf16[2,216,512]{2,1,0:T(8,128)(2,1)S(1)}, bf16[224,512]{1,0:T(8,128)(2,1)S(1)}, bf16[2,216,512]{2,1,0:T(8,128)(2,1)S(1)}, bf16[2,1536,216]{...) custom-call(bf16[864,512]{1,0:T(8,128)(2,1)S(1)} %bitcast.27, ...), custom_call_target="tpu_custom_call" | custom-call | flops 10000000000 | bytes 4194304 | tf_op jit(solution)/shard_map/fine_forward_1/pallas_call | solution.py:429
  32.3 0.0 copy-start.4
  32.4 0.4 pad_maximum_fusion.1
  32.8 0.3 copy.14
  33.1 0.1 collective-permute-start.7
  33.2 0.3 copy-done.4
  33.5 0.1 edges.3
  33.6 3.7 %collective-permute-start.8 = (bf16[216,512]{1,0:T(8,128)(2,1)S(1)}, bf16[216,512]{1,0:T(8,128)(2,1)S(1)}, u32[]{:S(2)}, u32[]{:S(2)}) collective-permute-start(bf16[216,512]{1,0:T(8,128)(2,1)S(1)} %get-tuple-element.90), channel_id=1, source_target_pairs={{0,15},{1,0},{2,1},{3,2},{4,3},{5,4},{6,5},{7,6},{8,7},{9,8},{10,9... | collective-permute-start | bytes 663560 | tf_op jit(solution)/shard_map/ppermute | solution.py:538
  37.3 5.7 %collective-permute-start.9 = (bf16[162,512]{1,0:T(8,128)(2,1)S(1)}, bf16[162,512]{1,0:T(8,128)(2,1)S(1)}, u32[]{:S(2)}, u32[]{:S(2)}) collective-permute-start(bf16[162,512]{1,0:T(8,128)(2,1)S(1)} %get-tuple-element.91), channel_id=1, source_target_pairs={{0,112},{16,0},{32,16},{48,32},{64,48},{80,64},{96,80},{112,96},{1... | collective-permute-start | bytes 497672 | tf_op jit(solution)/shard_map/ppermute | solution.py:538
  43.0 0.2 collective-permute-start.10
  43.3 14.2 %coarse_both.1 = (bf16[1024,216]{1,0:T(8,128)(2,1)S(1)}, bf16[216,1024]{1,0:T(8,128)(2,1)S(1)}, bf16[864,512]{1,0:T(8,128)(2,1)S(1)}, bf16[216,512]{1,0:T(8,128)...) custom-call(bf16[2,216,512]{2,1,0:T(8,128)(2,1)S(1)} %get-tuple-element.70.y0_ref, ...), custom_call_target="tpu_custom_call" | custom-call | flops 20000000000 | bytes 4194304 | tf_op jit(solution)/shard_map/coarse_both/pallas_call | solution.py:429
  57.5 1.3 collective-permute-start.11
  58.8 3.0 %collective-permute-start.14 = (bf16[162,512]{1,0:T(8,128)(2,1)S(1)}, bf16[162,512]{1,0:T(8,128)(2,1)S(1)}, u32[]{:S(2)}, u32[]{:S(2)}) collective-permute-start(bf16[162,512]{1,0:T(8,128)(2,1)S(1)} %get-tuple-element.102), channel_id=1, source_target_pairs={{0,16},{16,32},{32,48},{48,64},{64,80},{80,96},{96,112},{112,0},{1... | collective-permute-start | bytes 497672 | tf_op jit(solution)/shard_map/ppermute | solution.py:538
  61.8 0.1 collective-permute-start.15
  61.9 0.7 coarse_out.1
  62.6 0.9 normed.1
  63.6 4.3 %fine_backward_1.1 = (bf16[2,1536,256]{2,1,0:T(8,128)(2,1)S(1)}, bf16[2,216,512]{2,1,0:T(8,128)(2,1)S(1)}) custom-call(bf16[864,512]{1,0:T(8,128)(2,1)S(1)} %get-tuple-element.100.refs_0_, bf16[216,512]{1,0:T(8,128)(2,1)S(1)} %collective-permute-done.11.refs_1_, bf16[864,512]{1,0:T(8,128)(2,1)S(1)} %bitcast.29, ...), custom_call_target="tpu_custom_call" | custom-call | flops 10000000000 | bytes 4194304 | tf_op jit(solution)/shard_map/fine_backward_1/pallas_call | solution.py:429
  67.8 2.8 %collective-permute-done.15.refs_3_ = bf16[54,512]{1,0:T(8,128)(2,1)S(1)} collective-permute-done((bf16[54,512]{1,0:T(8,128)(2,1)S(1)}, bf16[54,512]{1,0:T(8,128)(2,1)S(1)}, u32[]{:S(2)}, u32[]{:S(2)}) %collective-permute-start.15) | collective-permute-done | bytes 55328 | tf_op jit(solution)/shard_map/ppermute | solution.py:548
  70.7 6.6 %fine_backward_0.1 = (bf16[2,1536,256]{2,1,0:T(8,128)(2,1)S(1)}, bf16[2,216,512]{2,1,0:T(8,128)(2,1)S(1)}, bf16[512,1024]{1,0:T(8,128)(2,1)S(1)}, bf16[512,1024]{1,0:T(8,128)(2,1)S(1)}) custom-call(bf16[864,512]{1,0:T(8,128)(2,1)S(1)} %get-tuple-element.100.refs_0_, bf16[216,512]{1,0:T(8,128)(2,1)S(1)} %collective-permute-done.11.refs_1_, ...), custom_call_target="tpu_custom_call" | custom-call | flops 10000000000 | bytes 4194304 | tf_op jit(solution)/shard_map/fine_backward_0/pallas_call | solution.py:429
  77.2 0.4 collective-permute-start.16
  77.7 2.8 %fine_input.1 = (bf16[2,216,512]{2,1,0:T(8,128)(2,1)S(1)}, bf16[2,216,512]{2,1,0:T(8,128)(2,1)S(1)}, bf16[216,512]{1,0:T(8,128)(2,1)S(1)}, bf16[162,512]{1,0:T(8,128)(2,1)S(1)}, bf16[54,512]{1,0:T(8,128)(2,1)S(1)}) custom-call(bf16[2,1536,256]{2,1,0:T(8,128)(2,1)S(1)} %get-tuple-element.121.gq0_ref, ...), custom_call_target="tpu_custom_call" | custom-call | flops 6000000000 | bytes 4194304 | tf_op jit(solution)/shard_map/fine_input/pallas_call | solution.py:429
  80.5 0.0 copy-start.10
  80.5 0.8 copy-done.10
  81.3 0.8 copy-done.12
  82.0 1.4 %fusion = bf16[64,8,1024]{2,1,0:T(8,128)(2,1)} fusion(bf16[512,1024]{1,0:T(8,128)(2,1)S(1)} %collective-permute-done.16, bf16[512,1024]{1,0:T(8,128)(2,1)S(1)} %get-tuple-element.124), kind=kLoop, calls=%fused_computation.2 | loop fusion | flops 2097152 | bytes 3145728 | tf_op jit(solution)/shard_map/reshape | solution.py:563
  83.4 5.9 %all-to-all-start = ((bf16[64,8,1024]{2,1,0:T(8,128)(2,1)}), bf16[64,8,1024]{2,1,0:T(8,128)(2,1)S(1)}, u32[]{:S(2)}, u32[]{:S(2)}) async-start(bf16[64,8,1024]{2,1,0:T(8,128)(2,1)} %fusion), calls=%async_computation | async-start | bytes 2097152 | tf_op jit(solution)/shard_map/all_to_all | solution.py:563
  89.3 0.1 fusion.2
  89.4 0.0 copy-start.11
  89.4 0.0 copy-start.13
  89.5 0.2 copy.17
  89.7 2.6 %collective-permute-start.12 = (bf16[6,3,6,1024]{3,1,0,2:T(4,128)(2,1)S(1)}, bf16[6,3,6,1024]{3,1,0,2:T(4,128)(2,1)S(1)}, u32[]{:S(2)}, u32[]{:S(2)}) collective-permute-start(bf16[6,3,6,1024]{3,1,0,2:T(4,128)(2,1)S(1)} %copy.17), channel_id=1, source_target_pairs={{0,16},{16,32},{32,48},{48,64},{64,80},{80,96},{96,112},{112,0},{1... | collective-permute-start | bytes 663560 | tf_op jit(solution)/shard_map/ppermute | solution.py:538
  92.2 19.9 %collective-permute-done.12 = bf16[6,3,6,1024]{3,1,0,2:T(4,128)(2,1)S(1)} collective-permute-done((bf16[6,3,6,1024]{3,1,0,2:T(4,128)(2,1)S(1)}, bf16[6,3,6,1024]{3,1,0,2:T(4,128)(2,1)S(1)}, u32[]{:S(2)}, u32[]{:S(2)}) %collective-permute-start.12) | collective-permute-done | bytes 221216 | tf_op jit(solution)/shard_map/ppermute | solution.py:538
  112.2 0.1 constant_dynamic-update-slice_fusion
  112.3 0.2 copy_dynamic-update-slice_fusion
  112.5 0.9 fusion.1
  113.4 2.1 %collective-permute-start.13 = (bf16[3,3,12,1024]{3,1,0,2:T(4,128)(2,1)}, bf16[3,3,12,1024]{3,1,0,2:T(4,128)(2,1)S(1)}, u32[]{:S(2)}, u32[]{:S(2)}) collective-permute-start(bf16[3,3,12,1024]{3,1,0,2:T(4,128)(2,1)} %get-tuple-element.135), channel_id=1, source_target_pairs={{0,1},{1,2},{2,3},{3,4},{4,5},{5,6},{6,7},{7,8},{8,9},{9,10},{10,1... | collective-permute-start | bytes 663560 | tf_op jit(solution)/shard_map/ppermute | solution.py:538
  115.6 0.0 collective-permute-start.17
  115.6 4.0 %collective-permute-start.19 = (bf16[54,512]{1,0:T(8,128)(2,1)S(1)}, bf16[54,512]{1,0:T(8,128)(2,1)S(1)}, u32[]{:S(2)}, u32[]{:S(2)}) collective-permute-start(bf16[54,512]{1,0:T(8,128)(2,1)S(1)} %get-tuple-element.133), channel_id=1, source_target_pairs={{0,17},{1,18},{2,19},{3,20},{4,21},{5,22},{6,23},{7,24},{8,25},{9,... | collective-permute-start | bytes 165896 | tf_op jit(solution)/shard_map/ppermute | solution.py:548
  119.6 0.2 convert_reduce_fusion
  119.8 2.0 %collective-permute-done.17.lat_ref = bf16[216,512]{1,0:T(8,128)(2,1)S(1)} collective-permute-done((bf16[216,512]{1,0:T(8,128)(2,1)S(1)}, bf16[216,512]{1,0:T(8,128)(2,1)S(1)}, u32[]{:S(2)}, u32[]{:S(2)}) %collective-permute-start.17) | collective-permute-done | bytes 221216 | tf_op jit(solution)/shard_map/ppermute | solution.py:538
  121.8 4.9 %collective-permute-done.18.lon_ref = bf16[162,512]{1,0:T(8,128)(2,1)S(1)} collective-permute-done((bf16[162,512]{1,0:T(8,128)(2,1)S(1)}, bf16[162,512]{1,0:T(8,128)(2,1)S(1)}, u32[]{:S(2)}, u32[]{:S(2)}) %collective-permute-start.18) | collective-permute-done | bytes 165920 | tf_op jit(solution)/shard_map/ppermute | solution.py:538
  126.7 1.5 %collective-permute-done.19.corner_ref = bf16[54,512]{1,0:T(8,128)(2,1)S(1)} collective-permute-done((bf16[54,512]{1,0:T(8,128)(2,1)S(1)}, bf16[54,512]{1,0:T(8,128)(2,1)S(1)}, u32[]{:S(2)}, u32[]{:S(2)}) %collective-permute-start.19) | collective-permute-done | bytes 55328 | tf_op jit(solution)/shard_map/ppermute | solution.py:548
  128.3 0.2 collective-permute-start.20
  128.4 1.3 assemble.1
  129.7 1.2 maximum_bitcast_fusion
  131.0 0.6 pad_maximum_fusion.2
  (43 shorter events, 0.1 us)
Async XLA Ops:
  0.6 1.2 copy-start.2
  1.8 10.9 %copy-start.1 = (bf16[512,2048]{1,0:T(8,128)(2,1)S(1)}, bf16[512,2048]{1,0:T(8,128)(2,1)}, u32[]{:S(2)}) copy-start(bf16[512,2048]{1,0:T(8,128)(2,1)} %w_ref.3) | copy-start | bytes 6291460
  1.9 11.3 %collective-permute-start = (bf16[216,512]{1,0:T(8,128)(2,1)S(1)}, bf16[216,512]{1,0:T(8,128)(2,1)S(1)}, u32[]{:S(2)}, u32[]{:S(2)}) collective-permute-start(bf16[216,512]{1,0:T(8,128)(2,1)S(1)} %get-tuple-element.69), channel_id=1, source_target_pairs={{0,15},{1,0},{2,1},{3,2},{4,3},{5,4},{6,5},{7,6},{8,7},{9,8},{10,9... | collective-permute-start | bytes 663560 | tf_op jit(solution)/shard_map/ppermute | solution.py:538
  3.4 24.7 %collective-permute-start.1 = (bf16[162,512]{1,0:T(8,128)(2,1)S(1)}, bf16[162,512]{1,0:T(8,128)(2,1)S(1)}, u32[]{:S(2)}, u32[]{:S(2)}) collective-permute-start(bf16[162,512]{1,0:T(8,128)(2,1)S(1)} %get-tuple-element.71), channel_id=1, source_target_pairs={{0,112},{16,0},{32,16},{48,32},{64,48},{80,64},{96,80},{112,96},{1... | collective-permute-start | bytes 497672 | tf_op jit(solution)/shard_map/ppermute | solution.py:538
  9.5 18.5 %collective-permute-start.2 = (bf16[54,512]{1,0:T(8,128)(2,1)S(1)}, bf16[54,512]{1,0:T(8,128)(2,1)S(1)}, u32[]{:S(2)}, u32[]{:S(2)}) collective-permute-start(bf16[54,512]{1,0:T(8,128)(2,1)S(1)} %get-tuple-element.72), channel_id=1, source_target_pairs={{0,127},{1,112},{2,113},{3,114},{4,115},{5,116},{6,117},{7,118},{8... | collective-permute-start | bytes 165896 | tf_op jit(solution)/shard_map/ppermute | solution.py:548
  12.7 1.1 copy-start.14
  12.7 4.8 %copy-start.3 = (bf16[24,12,3,512]{3,0,2,1:T(8,128)(2,1)S(1)}, bf16[24,12,3,512]{3,0,2,1:T(8,128)(2,1)}, u32[]{:S(2)}) copy-start(bf16[24,12,3,512]{3,0,2,1:T(8,128)(2,1)} %param.11) | copy-start | bytes 2654212
  12.7 4.8 %copy-start.7 = (f32[512]{0:T(512)S(1)}, f32[512]{0:T(512)}, u32[]{:S(2)}) copy-start(f32[512]{0:T(512)} %param.13) | copy-start | bytes 6148
  12.7 4.8 %copy-start.9 = (f32[8]{0:T(128)S(1)}, f32[8]{0:T(128)}, u32[]{:S(2)}) copy-start(f32[8]{0:T(128)} %refs_11_.3) | copy-start | bytes 100
  14.0 10.7 %collective-permute-start.5 = (bf16[6,3,6,1024]{3,1,0,2:T(4,128)(2,1)S(1)}, bf16[6,3,6,1024]{3,1,0,2:T(4,128)(2,1)S(1)}, u32[]{:S(2)}, u32[]{:S(2)}) collective-permute-start(bf16[6,3,6,1024]{3,1,0,2:T(4,128)(2,1)S(1)} %get-tuple-element.142), channel_id=1, source_target_pairs={{0,112},{16,0},{32,16},{48,32},{64,48},{80,64},{96,80},{112,96},{1... | collective-permute-start | bytes 663560 | tf_op jit(solution)/shard_map/ppermute | solution.py:538
  21.9 11.2 %collective-permute-start.3 = (bf16[162,512]{1,0:T(8,128)(2,1)S(1)}, bf16[162,512]{1,0:T(8,128)(2,1)S(1)}, u32[]{:S(2)}, u32[]{:S(2)}) collective-permute-start(bf16[162,512]{1,0:T(8,128)(2,1)S(1)} %get-tuple-element.76), channel_id=1, source_target_pairs={{0,112},{16,0},{32,16},{48,32},{64,48},{80,64},{96,80},{112,96},{1... | collective-permute-start | bytes 497672 | tf_op jit(solution)/shard_map/ppermute | solution.py:538
  22.0 11.1 %collective-permute-start.4 = (bf16[54,512]{1,0:T(8,128)(2,1)S(1)}, bf16[54,512]{1,0:T(8,128)(2,1)S(1)}, u32[]{:S(2)}, u32[]{:S(2)}) collective-permute-start(bf16[54,512]{1,0:T(8,128)(2,1)S(1)} %get-tuple-element.77), channel_id=1, source_target_pairs={{0,127},{1,112},{2,113},{3,114},{4,115},{5,116},{6,117},{7,118},{8... | collective-permute-start | bytes 165896 | tf_op jit(solution)/shard_map/ppermute | solution.py:548
  25.1 18.2 %slice-start = ((s8[8388608]{0:T(1024)(128)(4,1)}), s8[4194304]{0:T(1024)(128)(4,1)S(1)}, s32[]{:S(2)}) async-start(s8[8388608]{0:T(1024)(128)(4,1)} %bitcast.21), calls=%async_computation.1 | async-start | bytes 8388608
  25.3 7.1 %collective-permute-start.6 = (bf16[3,3,12,1024]{3,1,0,2:T(4,128)(2,1)S(1)}, bf16[3,3,12,1024]{3,1,0,2:T(4,128)(2,1)S(1)}, u32[]{:S(2)}, u32[]{:S(2)}) collective-permute-start(bf16[3,3,12,1024]{3,1,0,2:T(4,128)(2,1)S(1)} %get-tuple-element.140), channel_id=1, source_target_pairs={{0,15},{1,0},{2,1},{3,2},{4,3},{5,4},{6,5},{7,6},{8,7},{9,8},{10,9... | collective-permute-start | bytes 663560 | tf_op jit(solution)/shard_map/ppermute | solution.py:538
  28.1 15.2 %slice-start.1 = ((s8[8388608]{0:T(1024)(128)(4,1)}), s8[4194304]{0:T(1024)(128)(4,1)S(1)}, s32[]{:S(2)}) async-start(s8[8388608]{0:T(1024)(128)(4,1)} %bitcast.21), calls=%async_computation.2 | async-start | bytes 8388608
  32.3 1.2 copy-start.4
  33.1 10.1 %collective-permute-start.7 = (bf16[224,512]{1,0:T(8,128)(2,1)S(1)}, bf16[224,512]{1,0:T(8,128)(2,1)S(1)}, u32[]{:S(2)}, u32[]{:S(2)}) collective-permute-start(bf16[224,512]{1,0:T(8,128)(2,1)S(1)} %get-tuple-element.80), channel_id=1, source_target_pairs={{0,15},{1,0},{2,1},{3,2},{4,3},{5,4},{6,5},{7,6},{8,7},{9,8},{10,9... | collective-permute-start | bytes 688136 | tf_op jit(solution)/shard_map/ppermute | solution.py:538
  33.5 9.7 %copy-start = (bf16[2048,1024]{1,0:T(8,128)(2,1)S(1)}, bf16[2048,1024]{1,0:T(8,128)(2,1)}, u32[]{:S(2)}) copy-start(bf16[2048,1024]{1,0:T(8,128)(2,1)} %mw_ref.1) | copy-start | bytes 12582916
  33.5 9.7 %copy-start.5 = (f32[2048]{0:T(1024)S(1)}, f32[2048]{0:T(1024)}, u32[]{:S(2)}) copy-start(f32[2048]{0:T(1024)} %param.15) | copy-start | bytes 24580
  33.5 9.7 %copy-start.6 = (f32[1024]{0:T(1024)S(1)}, f32[1024]{0:T(1024)}, u32[]{:S(2)}) copy-start(f32[1024]{0:T(1024)} %param.18) | copy-start | bytes 12292
  33.5 9.7 %copy-start.8 = (f32[16]{0:T(128)S(1)}, f32[16]{0:T(128)}, u32[]{:S(2)}) copy-start(f32[16]{0:T(128)} %scale_ref.1) | copy-start | bytes 196
  33.6 23.9 %collective-permute-start.8 = (bf16[216,512]{1,0:T(8,128)(2,1)S(1)}, bf16[216,512]{1,0:T(8,128)(2,1)S(1)}, u32[]{:S(2)}, u32[]{:S(2)}) collective-permute-start(bf16[216,512]{1,0:T(8,128)(2,1)S(1)} %get-tuple-element.90), channel_id=1, source_target_pairs={{0,15},{1,0},{2,1},{3,2},{4,3},{5,4},{6,5},{7,6},{8,7},{9,8},{10,9... | collective-permute-start | bytes 663560 | tf_op jit(solution)/shard_map/ppermute | solution.py:538
  37.3 20.2 %collective-permute-start.9 = (bf16[162,512]{1,0:T(8,128)(2,1)S(1)}, bf16[162,512]{1,0:T(8,128)(2,1)S(1)}, u32[]{:S(2)}, u32[]{:S(2)}) collective-permute-start(bf16[162,512]{1,0:T(8,128)(2,1)S(1)} %get-tuple-element.91), channel_id=1, source_target_pairs={{0,112},{16,0},{32,16},{48,32},{64,48},{80,64},{96,80},{112,96},{1... | collective-permute-start | bytes 497672 | tf_op jit(solution)/shard_map/ppermute | solution.py:538
  43.0 14.5 %collective-permute-start.10 = (bf16[54,512]{1,0:T(8,128)(2,1)S(1)}, bf16[54,512]{1,0:T(8,128)(2,1)S(1)}, u32[]{:S(2)}, u32[]{:S(2)}) collective-permute-start(bf16[54,512]{1,0:T(8,128)(2,1)S(1)} %get-tuple-element.92), channel_id=1, source_target_pairs={{0,127},{1,112},{2,113},{3,114},{4,115},{5,116},{6,117},{7,118},{8... | collective-permute-start | bytes 165896 | tf_op jit(solution)/shard_map/ppermute | solution.py:548
  57.5 6.1 %collective-permute-start.11 = (bf16[216,512]{1,0:T(8,128)(2,1)S(1)}, bf16[216,512]{1,0:T(8,128)(2,1)S(1)}, u32[]{:S(2)}, u32[]{:S(2)}) collective-permute-start(bf16[216,512]{1,0:T(8,128)(2,1)S(1)} %get-tuple-element.93), channel_id=1, source_target_pairs={{0,1},{1,2},{2,3},{3,4},{4,5},{5,6},{6,7},{7,8},{8,9},{9,10},{10,1... | collective-permute-start | bytes 663560 | tf_op jit(solution)/shard_map/ppermute | solution.py:538
  58.8 11.8 %collective-permute-start.14 = (bf16[162,512]{1,0:T(8,128)(2,1)S(1)}, bf16[162,512]{1,0:T(8,128)(2,1)S(1)}, u32[]{:S(2)}, u32[]{:S(2)}) collective-permute-start(bf16[162,512]{1,0:T(8,128)(2,1)S(1)} %get-tuple-element.102), channel_id=1, source_target_pairs={{0,16},{16,32},{32,48},{48,64},{64,80},{80,96},{96,112},{112,0},{1... | collective-permute-start | bytes 497672 | tf_op jit(solution)/shard_map/ppermute | solution.py:538
  61.8 8.9 %collective-permute-start.15 = (bf16[54,512]{1,0:T(8,128)(2,1)S(1)}, bf16[54,512]{1,0:T(8,128)(2,1)S(1)}, u32[]{:S(2)}, u32[]{:S(2)}) collective-permute-start(bf16[54,512]{1,0:T(8,128)(2,1)S(1)} %get-tuple-element.103), channel_id=1, source_target_pairs={{0,17},{1,18},{2,19},{3,20},{4,21},{5,22},{6,23},{7,24},{8,25},{9,... | collective-permute-start | bytes 165896 | tf_op jit(solution)/shard_map/ppermute | solution.py:548
  77.2 4.8 %collective-permute-start.16 = (bf16[512,1024]{1,0:T(8,128)(2,1)S(1)}, bf16[512,1024]{1,0:T(8,128)(2,1)S(1)}, u32[]{:S(2)}, u32[]{:S(2)}) collective-permute-start(bf16[512,1024]{1,0:T(8,128)(2,1)S(1)} %get-tuple-element.119), channel_id=1, source_target_pairs={{0,1},{1,0},{2,3},{3,2},{4,5},{5,4},{6,7},{7,6},{8,9},{9,8},{10,11... | collective-permute-start | bytes 3145736 | tf_op jit(solution)/shard_map/ppermute | solution.py:614
  80.5 0.8 copy-start.10
  81.3 0.8 copy-start.12
  83.4 36.2 %all-to-all-start = ((bf16[64,8,1024]{2,1,0:T(8,128)(2,1)}), bf16[64,8,1024]{2,1,0:T(8,128)(2,1)S(1)}, u32[]{:S(2)}, u32[]{:S(2)}) async-start(bf16[64,8,1024]{2,1,0:T(8,128)(2,1)} %fusion), calls=%async_computation | async-start | bytes 2097152 | tf_op jit(solution)/shard_map/all_to_all | solution.py:563
  89.4 39.0 %copy-start.11 = (bf16[2,216,512]{2,1,0:T(8,128)(2,1)S(1)}, bf16[2,216,512]{2,1,0:T(8,128)(2,1)}, u32[]{:S(2)}) copy-start(bf16[2,216,512]{2,1,0:T(8,128)(2,1)} %copy-done.10) | copy-start | bytes 1327108
  89.4 39.0 %copy-start.13 = (bf16[2,216,512]{2,1,0:T(8,128)(2,1)S(1)}, bf16[2,216,512]{2,1,0:T(8,128)(2,1)}, u32[]{:S(2)}) copy-start(bf16[2,216,512]{2,1,0:T(8,128)(2,1)} %copy-done.12) | copy-start | bytes 1327108
  89.7 22.5 %collective-permute-start.12 = (bf16[6,3,6,1024]{3,1,0,2:T(4,128)(2,1)S(1)}, bf16[6,3,6,1024]{3,1,0,2:T(4,128)(2,1)S(1)}, u32[]{:S(2)}, u32[]{:S(2)}) collective-permute-start(bf16[6,3,6,1024]{3,1,0,2:T(4,128)(2,1)S(1)} %copy.17), channel_id=1, source_target_pairs={{0,16},{16,32},{32,48},{48,64},{64,80},{80,96},{96,112},{112,0},{1... | collective-permute-start | bytes 663560 | tf_op jit(solution)/shard_map/ppermute | solution.py:538
  113.4 6.3 %collective-permute-start.13 = (bf16[3,3,12,1024]{3,1,0,2:T(4,128)(2,1)}, bf16[3,3,12,1024]{3,1,0,2:T(4,128)(2,1)S(1)}, u32[]{:S(2)}, u32[]{:S(2)}) collective-permute-start(bf16[3,3,12,1024]{3,1,0,2:T(4,128)(2,1)} %get-tuple-element.135), channel_id=1, source_target_pairs={{0,1},{1,2},{2,3},{3,4},{4,5},{5,6},{6,7},{7,8},{8,9},{9,10},{10,1... | collective-permute-start | bytes 663560 | tf_op jit(solution)/shard_map/ppermute | solution.py:538
  115.6 6.2 %collective-permute-start.17 = (bf16[216,512]{1,0:T(8,128)(2,1)S(1)}, bf16[216,512]{1,0:T(8,128)(2,1)S(1)}, u32[]{:S(2)}, u32[]{:S(2)}) collective-permute-start(bf16[216,512]{1,0:T(8,128)(2,1)S(1)} %get-tuple-element.129), channel_id=1, source_target_pairs={{0,1},{1,2},{2,3},{3,4},{4,5},{5,6},{6,7},{7,8},{8,9},{9,10},{10,1... | collective-permute-start | bytes 663560 | tf_op jit(solution)/shard_map/ppermute | solution.py:538
  115.6 11.1 %collective-permute-start.18 = (bf16[162,512]{1,0:T(8,128)(2,1)S(1)}, bf16[162,512]{1,0:T(8,128)(2,1)S(1)}, u32[]{:S(2)}, u32[]{:S(2)}) collective-permute-start(bf16[162,512]{1,0:T(8,128)(2,1)S(1)} %get-tuple-element.131), channel_id=1, source_target_pairs={{0,16},{16,32},{32,48},{48,64},{64,80},{80,96},{96,112},{112,0},{1... | collective-permute-start | bytes 497672 | tf_op jit(solution)/shard_map/ppermute | solution.py:538
  115.6 12.7 %collective-permute-start.19 = (bf16[54,512]{1,0:T(8,128)(2,1)S(1)}, bf16[54,512]{1,0:T(8,128)(2,1)S(1)}, u32[]{:S(2)}, u32[]{:S(2)}) collective-permute-start(bf16[54,512]{1,0:T(8,128)(2,1)S(1)} %get-tuple-element.133), channel_id=1, source_target_pairs={{0,17},{1,18},{2,19},{3,20},{4,21},{5,22},{6,23},{7,24},{8,25},{9,... | collective-permute-start | bytes 165896 | tf_op jit(solution)/shard_map/ppermute | solution.py:548
  128.3 2.7 %collective-permute-start.20 = (f32[4,1024]{1,0:T(4,128)S(1)}, f32[4,1024]{1,0:T(4,128)S(1)}, u32[]{:S(2)}, u32[]{:S(2)}) collective-permute-start(f32[4,1024]{1,0:T(4,128)S(1)} %slice_select_fusion), channel_id=1, source_target_pairs={{0,1},{1,0},{2,3},{3,2},{4,5},{5,4},{6,7},{7,6},{8,9},{9,8},{10,11... | collective-permute-start | bytes 49160 | tf_op jit(solution)/shard_map/ppermute | solution.py:570
where the time goes:
time: 132 us
  starting transfers between devices  49.1 us (37%)
  Pallas kernels  40.1 us (30%)
  waiting for transfers between devices  31.3 us (24%)
  local copies, waits for them, and re-layouts  5.91 us (4%)
  other arithmetic  4.19 us (3%)
    pallas_call x12, Pallas kernels, call(): pl.pallas_call(kernel, out_shape=[jax.ShapeDtypeStruct(shape, kind) for s...  40.1 us
    ppermute x14, starting transfers between devices, moved(): return lax.ppermute(block, axis, ring(lax.axis_size(axis), step))  32.5 us
    ppermute x14, waiting for transfers between devices, moved(): return lax.ppermute(block, axis, ring(lax.axis_size(axis), step))  26.9 us
    ppermute x5, starting transfers between devices, moved_both(): return lax.ppermute(block, ('lon', *LAT_AXES), route)  10.2 us
    all_to_all x1, starting transfers between devices, chip_sum(): pieces = lax.all_to_all(part.reshape(64, 8, 2 * D1), ('lon', 'chip'), 0, 0)  5.88 us
    ppermute x5, waiting for transfers between devices, moved_both(): return lax.ppermute(block, ('lon', *LAT_AXES), route)  4.35 us
    unnamed x36, local copies, waits for them, and re-layouts  3.89 us
  transfers between devices with their start and end apart: 22, of which 5 were waited for; matrix products, arithmetic and copies ran while one was open for 3% of the time, Pallas kernels for 25%

commit v1 on v0

--- a/solution.py
+++ b/solution.py
@@ -605,6 +605,7 @@
     coarse_out, glat, normt0, normt1 = lax.optimization_barrier((coarse_out, glat, normt0, normt1))
     coarse_out = half_moved(coarse_out.reshape(LAT // 2, LEV, LON // 2, D2), "lon", 2, 1)
     gq1, e1 = fine_backward(1, (grad, glat, cot_tile, *cot_edges), saved1[1:], fine_weights, fine_scales)
+    gq1, coarse_out = lax.optimization_barrier((gq1, coarse_out))
     own, other = jnp.split(coarse_out, 2, 0)
     other = moved(other, LAT_AXES, 1)
     gq0, e0, keep, send = fine_backward(
@@ -620,9 +621,9 @@
     part = (keep.astype(F32) + sent.astype(F32)).astype(BF16)
     total = chip_sum(part)
     share = own_rows(total, core[0])
-    lat, lon, corner, other = (after(block, total) for block in (lat, lon, corner, other))
+    lat, lon, corner = (after(block, total) for block in (lat, lon, corner))
     grad_input = assemble((g0, g1, lat, lon, corner)).reshape(LAT, LEV, LON, D1)
-    coarse_out = jnp.concatenate([other, own], 0)
+    coarse_out = jnp.concatenate([after(other, total), own], 0)
     return coarse_out.transpose(2, 0, 1, 3), grad_input.transpose(2, 0, 1, 3), share
 
 

time: 132 us -> 126 us (0.955)
  waiting for transfers between devices: 31.3 us -> 22.7 us
  starting transfers between devices: 49.1 us -> 52 us
  local copies, waits for them, and re-layouts: 5.91 us -> 4.33 us
    ppermute x14, waiting for transfers between devices: 26.9 us -> 8.91 us  [moved(): return lax.ppermute(block, axis, ring(lax.axis_size(axis), step))]
    all_to_all x1, waiting for transfers between devices: 0.01 us -> 12.1 us  [chip_sum(): pieces = lax.all_to_all(part.reshape(64, 8, 2 * D1), ('lon', 'chip'), 0, 0)]
    ppermute x5, waiting for transfers between devices: 4.35 us -> 1.63 us  [moved_both(): return lax.ppermute(block, ('lon', *LAT_AXES), route)]
    ppermute x1, starting transfers between devices: 0.44 us -> 2.83 us  [on_device(): sent = lax.ppermute(send, 'core', [(0, 1), (1, 0)])]
    ppermute x1, starting transfers between devices: 0.16 us -> 2.26 us  [own_rows(): lax.ppermute(jnp.where(first, total[4:], total[:4]), 'core', [(0, 1), (1,...]
    unnamed x36 -> x32, local copies, waits for them, and re-layouts: 3.89 us -> 2.47 us
    ppermute x5, starting transfers between devices: 10.2 us -> 8.79 us  [moved_both(): return lax.ppermute(block, ('lon', *LAT_AXES), route)]
  transfers between devices with their start and end apart: 22 -> 22, of which waited for: 5 -> 4; matrix products, arithmetic and copies ran while one was open for 3% -> 4% of each run, Pallas kernels for 25% -> 27%
where the time goes in v1:
time: 126 us; the launch traced here: 125 us
  starting transfers between devices  52 us (41%)
  Pallas kernels  40.1 us (32%)
  waiting for transfers between devices  22.7 us (18%)
  other arithmetic  5.38 us (4%)
  local copies, waits for them, and re-layouts  4.33 us (3%)
    pallas_call x12, Pallas kernels, call(): pl.pallas_call(kernel, out_shape=[jax.ShapeDtypeStruct(shape, kind) for s...  40.1 us
    ppermute x14, starting transfers between devices, moved(): return lax.ppermute(block, axis, ring(lax.axis_size(axis), step))  33.4 us
    all_to_all x1, waiting for transfers between devices, chip_sum(): pieces = lax.all_to_all(part.reshape(64, 8, 2 * D1), ('lon', 'chip'), 0, 0)  12.1 us
    ppermute x14, waiting for transfers between devices, moved(): return lax.ppermute(block, axis, ring(lax.axis_size(axis), step))  8.91 us
    ppermute x5, starting transfers between devices, moved_both(): return lax.ppermute(block, ('lon', *LAT_AXES), route)  8.79 us
    all_to_all x1, starting transfers between devices, chip_sum(): pieces = lax.all_to_all(part.reshape(64, 8, 2 * D1), ('lon', 'chip'), 0, 0)  4.78 us
    ppermute x1, starting transfers between devices, on_device(): sent = lax.ppermute(send, 'core', [(0, 1), (1, 0)])  2.83 us
  transfers between devices with their start and end apart: 22, of which 4 were waited for; matrix products, arithmetic and copies ran while one was open for 4% of the time, Pallas kernels for 27%

profile of v1, /device:TPU:1, one launch (start us, length us, event | category | flops | bytes accessed | tf_op | source)
XLA Modules:
  0.0 125.5 jit_solution(8133111151765223554)
XLA Ops:
  0.6 0.0 copy-start.2
  0.6 1.2 copy-done.2
  1.8 0.1 edges.2
  1.9 1.5 %collective-permute-start = (bf16[216,512]{1,0:T(8,128)(2,1)S(1)}, bf16[216,512]{1,0:T(8,128)(2,1)S(1)}, u32[]{:S(2)}, u32[]{:S(2)}) collective-permute-start(bf16[216,512]{1,0:T(8,128)(2,1)S(1)} %get-tuple-element.71), channel_id=1, source_target_pairs={{0,15},{1,0},{2,1},{3,2},{4,3},{5,4},{6,5},{7,6},{8,7},{9,8},{10,9... | collective-permute-start | bytes 663560 | tf_op jit(solution)/shard_map/ppermute | solution.py:538
  3.4 6.1 %collective-permute-start.1 = (bf16[162,512]{1,0:T(8,128)(2,1)S(1)}, bf16[162,512]{1,0:T(8,128)(2,1)S(1)}, u32[]{:S(2)}, u32[]{:S(2)}) collective-permute-start(bf16[162,512]{1,0:T(8,128)(2,1)S(1)} %get-tuple-element.73), channel_id=1, source_target_pairs={{0,112},{16,0},{32,16},{48,32},{64,48},{80,64},{96,80},{112,96},{1... | collective-permute-start | bytes 497672 | tf_op jit(solution)/shard_map/ppermute | solution.py:538
  9.5 3.2 %collective-permute-start.2 = (bf16[54,512]{1,0:T(8,128)(2,1)S(1)}, bf16[54,512]{1,0:T(8,128)(2,1)S(1)}, u32[]{:S(2)}, u32[]{:S(2)}) collective-permute-start(bf16[54,512]{1,0:T(8,128)(2,1)S(1)} %get-tuple-element.74), channel_id=1, source_target_pairs={{0,127},{1,112},{2,113},{3,114},{4,115},{5,116},{6,117},{7,118},{8... | collective-permute-start | bytes 165896 | tf_op jit(solution)/shard_map/ppermute | solution.py:548
  12.7 0.0 copy-start.9
  12.7 0.5 turn.1.refs_2_.refs_5_
  13.2 0.0 collective-permute-done.refs_1_
  13.2 0.6 copy-done.12
  13.8 0.2 fusion.4
  14.0 3.5 %collective-permute-start.5 = (bf16[6,3,6,1024]{3,1,0,2:T(4,128)(2,1)S(1)}, bf16[6,3,6,1024]{3,1,0,2:T(4,128)(2,1)S(1)}, u32[]{:S(2)}, u32[]{:S(2)}) collective-permute-start(bf16[6,3,6,1024]{3,1,0,2:T(4,128)(2,1)S(1)} %get-tuple-element.146), channel_id=1, source_target_pairs={{0,112},{16,0},{32,16},{48,32},{64,48},{80,64},{96,80},{112,96},{1... | collective-permute-start | bytes 663560 | tf_op jit(solution)/shard_map/ppermute | solution.py:538
  17.4 4.4 %fine_forward_0.1 = (bf16[2,216,512]{2,1,0:T(8,128)(2,1)S(1)}, bf16[112,512]{1,0:T(8,128)(2,1)S(1)}, bf16[162,512]{1,0:T(8,128)(2,1)S(1)}, bf16[54,512]{1,0:T(8,...) custom-call(bf16[864,512]{1,0:T(8,128)(2,1)S(1)} %bitcast.26, ...), custom_call_target="tpu_custom_call" | custom-call | flops 10000000000 | bytes 4194304 | tf_op jit(solution)/shard_map/fine_forward_0/pallas_call | solution.py:429
  21.9 0.1 collective-permute-start.3
  22.0 2.7 %collective-permute-start.4 = (bf16[54,512]{1,0:T(8,128)(2,1)S(1)}, bf16[54,512]{1,0:T(8,128)(2,1)S(1)}, u32[]{:S(2)}, u32[]{:S(2)}) collective-permute-start(bf16[54,512]{1,0:T(8,128)(2,1)S(1)} %get-tuple-element.79), channel_id=1, source_target_pairs={{0,127},{1,112},{2,113},{3,114},{4,115},{5,116},{6,117},{7,118},{8... | collective-permute-start | bytes 165896 | tf_op jit(solution)/shard_map/ppermute | solution.py:548
  24.7 0.0 collective-permute-done.5
  24.7 0.4 pad_maximum_fusion
  25.0 0.0 slice-start
  25.1 0.2 fusion.3
  25.3 2.8 %collective-permute-start.6 = (bf16[3,3,12,1024]{3,1,0,2:T(4,128)(2,1)S(1)}, bf16[3,3,12,1024]{3,1,0,2:T(4,128)(2,1)S(1)}, u32[]{:S(2)}, u32[]{:S(2)}) collective-permute-start(bf16[3,3,12,1024]{3,1,0,2:T(4,128)(2,1)S(1)} %get-tuple-element.144), channel_id=1, source_target_pairs={{0,15},{1,0},{2,1},{3,2},{4,3},{5,4},{6,5},{7,6},{8,7},{9,8},{10,9... | collective-permute-start | bytes 663560 | tf_op jit(solution)/shard_map/ppermute | solution.py:538
  28.0 4.3 %fine_forward_1.1 = (bf16[2,216,512]{2,1,0:T(8,128)(2,1)S(1)}, bf16[224,512]{1,0:T(8,128)(2,1)S(1)}, bf16[2,216,512]{2,1,0:T(8,128)(2,1)S(1)}, bf16[2,1536,216]{...) custom-call(bf16[864,512]{1,0:T(8,128)(2,1)S(1)} %bitcast.27, ...), custom_call_target="tpu_custom_call" | custom-call | flops 10000000000 | bytes 4194304 | tf_op jit(solution)/shard_map/fine_forward_1/pallas_call | solution.py:429
  32.3 0.0 copy-start.4
  32.3 0.4 pad_maximum_fusion.1
  32.7 0.3 copy.14
  33.1 0.0 collective-permute-done.4.corner_ref
  33.1 0.0 collective-permute-done.3.lon_ref
  33.1 0.1 collective-permute-start.7
  33.2 0.3 copy-done.4
  33.5 0.1 edges.3
  33.6 3.7 %collective-permute-start.8 = (bf16[216,512]{1,0:T(8,128)(2,1)S(1)}, bf16[216,512]{1,0:T(8,128)(2,1)S(1)}, u32[]{:S(2)}, u32[]{:S(2)}) collective-permute-start(bf16[216,512]{1,0:T(8,128)(2,1)S(1)} %get-tuple-element.93), channel_id=1, source_target_pairs={{0,15},{1,0},{2,1},{3,2},{4,3},{5,4},{6,5},{7,6},{8,7},{9,8},{10,9... | collective-permute-start | bytes 663560 | tf_op jit(solution)/shard_map/ppermute | solution.py:538
  37.3 5.7 %collective-permute-start.9 = (bf16[162,512]{1,0:T(8,128)(2,1)S(1)}, bf16[162,512]{1,0:T(8,128)(2,1)S(1)}, u32[]{:S(2)}, u32[]{:S(2)}) collective-permute-start(bf16[162,512]{1,0:T(8,128)(2,1)S(1)} %get-tuple-element.94), channel_id=1, source_target_pairs={{0,112},{16,0},{32,16},{48,32},{64,48},{80,64},{96,80},{112,96},{1... | collective-permute-start | bytes 497672 | tf_op jit(solution)/shard_map/ppermute | solution.py:538
  43.0 0.2 collective-permute-start.10
  43.2 14.2 %coarse_both.1 = (bf16[1024,216]{1,0:T(8,128)(2,1)S(1)}, bf16[216,1024]{1,0:T(8,128)(2,1)S(1)}, bf16[864,512]{1,0:T(8,128)(2,1)S(1)}, bf16[216,512]{1,0:T(8,128)...) custom-call(bf16[2,216,512]{2,1,0:T(8,128)(2,1)S(1)} %get-tuple-element.72.y0_ref, ...), custom_call_target="tpu_custom_call" | custom-call | flops 20000000000 | bytes 4194304 | tf_op jit(solution)/shard_map/coarse_both/pallas_call | solution.py:429
  57.4 0.0 collective-permute-done.10.refs_5_
  57.4 1.3 %collective-permute-start.11 = (bf16[216,512]{1,0:T(8,128)(2,1)S(1)}, bf16[216,512]{1,0:T(8,128)(2,1)S(1)}, u32[]{:S(2)}, u32[]{:S(2)}) collective-permute-start(bf16[216,512]{1,0:T(8,128)(2,1)S(1)} %get-tuple-element.96), channel_id=1, source_target_pairs={{0,1},{1,2},{2,3},{3,4},{4,5},{5,6},{6,7},{7,8},{8,9},{9,10},{10,1... | collective-permute-start | bytes 663560 | tf_op jit(solution)/shard_map/ppermute | solution.py:538
  58.8 3.0 %collective-permute-start.14 = (bf16[162,512]{1,0:T(8,128)(2,1)S(1)}, bf16[162,512]{1,0:T(8,128)(2,1)S(1)}, u32[]{:S(2)}, u32[]{:S(2)}) collective-permute-start(bf16[162,512]{1,0:T(8,128)(2,1)S(1)} %get-tuple-element.113), channel_id=1, source_target_pairs={{0,16},{16,32},{32,48},{48,64},{64,80},{80,96},{96,112},{112,0},{1... | collective-permute-start | bytes 497672 | tf_op jit(solution)/shard_map/ppermute | solution.py:538
  61.7 0.7 coarse_out.1
  62.5 0.9 normed.1
  63.4 0.1 fusion.2
  63.5 0.2 copy.17
  63.7 1.5 %collective-permute-start.12 = (bf16[6,3,6,1024]{3,1,0,2:T(4,128)(2,1)S(1)}, bf16[6,3,6,1024]{3,1,0,2:T(4,128)(2,1)S(1)}, u32[]{:S(2)}, u32[]{:S(2)}) collective-permute-start(bf16[6,3,6,1024]{3,1,0,2:T(4,128)(2,1)S(1)} %copy.17), channel_id=1, source_target_pairs={{0,16},{16,32},{32,48},{48,64},{64,80},{80,96},{96,112},{112,0},{1... | collective-permute-start | bytes 663560 | tf_op jit(solution)/shard_map/ppermute | solution.py:538
  65.2 4.2 %fine_backward_1.1 = (bf16[2,1536,256]{2,1,0:T(8,128)(2,1)S(1)}, bf16[2,216,512]{2,1,0:T(8,128)(2,1)S(1)}) custom-call(bf16[864,512]{1,0:T(8,128)(2,1)S(1)} %get-tuple-element.86.refs_0_, bf16[216,512]{1,0:T(8,128)(2,1)S(1)} %collective-permute-done.11.refs_1_, bf16[864,512]{1,0:T(8,128)(2,1)S(1)} %bitcast.29, ...), custom_call_target="tpu_custom_call" | custom-call | flops 10000000000 | bytes 4194304 | tf_op jit(solution)/shard_map/fine_backward_1/pallas_call | solution.py:429
  69.5 0.2 copy.18
  69.7 5.2 %collective-permute-done.12 = bf16[6,3,6,1024]{3,1,0,2:T(4,128)(2,1)S(1)} collective-permute-done((bf16[6,3,6,1024]{3,1,0,2:T(4,128)(2,1)S(1)}, bf16[6,3,6,1024]{3,1,0,2:T(4,128)(2,1)S(1)}, u32[]{:S(2)}, u32[]{:S(2)}) %collective-permute-start.12) | collective-permute-done | bytes 221216 | tf_op jit(solution)/shard_map/ppermute | solution.py:538
  74.9 1.2 pad_maximum_fusion.2
  76.1 6.6 %fine_backward_0.1 = (bf16[2,1536,256]{2,1,0:T(8,128)(2,1)S(1)}, bf16[2,216,512]{2,1,0:T(8,128)(2,1)S(1)}, bf16[512,1024]{1,0:T(8,128)(2,1)S(1)}, bf16[512,1024]{1,0:T(8,128)(2,1)S(1)}) custom-call(bf16[864,512]{1,0:T(8,128)(2,1)S(1)} %get-tuple-element.86.refs_0_, bf16[216,512]{1,0:T(8,128)(2,1)S(1)} %collective-permute-done.11.refs_1_, ...), custom_call_target="tpu_custom_call" | custom-call | flops 10000000000 | bytes 4194304 | tf_op jit(solution)/shard_map/fine_backward_0/pallas_call | solution.py:429
  82.6 2.8 %collective-permute-start.16 = (bf16[512,1024]{1,0:T(8,128)(2,1)S(1)}, bf16[512,1024]{1,0:T(8,128)(2,1)S(1)}, u32[]{:S(2)}, u32[]{:S(2)}) collective-permute-start(bf16[512,1024]{1,0:T(8,128)(2,1)S(1)} %get-tuple-element.123), channel_id=1, source_target_pairs={{0,1},{1,0},{2,3},{3,2},{4,5},{5,4},{6,7},{7,6},{8,9},{9,8},{10,11... | collective-permute-start | bytes 3145736 | tf_op jit(solution)/shard_map/ppermute | solution.py:615
  85.5 2.8 %fine_input.1 = (bf16[2,216,512]{2,1,0:T(8,128)(2,1)S(1)}, bf16[2,216,512]{2,1,0:T(8,128)(2,1)S(1)}, bf16[216,512]{1,0:T(8,128)(2,1)S(1)}, bf16[162,512]{1,0:T(8,128)(2,1)S(1)}, bf16[54,512]{1,0:T(8,128)(2,1)S(1)}) custom-call(bf16[2,1536,256]{2,1,0:T(8,128)(2,1)S(1)} %get-tuple-element.125.gq0_ref, ...), custom_call_target="tpu_custom_call" | custom-call | flops 6000000000 | bytes 4194304 | tf_op jit(solution)/shard_map/fine_input/pallas_call | solution.py:429
  88.3 0.0 copy-start.10
  88.3 1.4 %fusion = bf16[64,8,1024]{2,1,0:T(8,128)(2,1)} fusion(bf16[512,1024]{1,0:T(8,128)(2,1)S(1)} %collective-permute-done.16, bf16[512,1024]{1,0:T(8,128)(2,1)S(1)} %get-tuple-element.128), kind=kLoop, calls=%fused_computation.2 | loop fusion | flops 2097152 | bytes 3145728 | tf_op jit(solution)/shard_map/reshape | solution.py:563
  89.7 4.8 %all-to-all-start = ((bf16[64,8,1024]{2,1,0:T(8,128)(2,1)}), bf16[64,8,1024]{2,1,0:T(8,128)(2,1)S(1)}, u32[]{:S(2)}, u32[]{:S(2)}) async-start(bf16[64,8,1024]{2,1,0:T(8,128)(2,1)} %fusion), calls=%async_computation | async-start | bytes 2097152 | tf_op jit(solution)/shard_map/all_to_all | solution.py:563
  94.5 1.0 fusion.1
  95.5 1.5 %collective-permute-start.13 = (bf16[3,3,12,1024]{3,1,0,2:T(4,128)(2,1)}, bf16[3,3,12,1024]{3,1,0,2:T(4,128)(2,1)S(1)}, u32[]{:S(2)}, u32[]{:S(2)}) collective-permute-start(bf16[3,3,12,1024]{3,1,0,2:T(4,128)(2,1)} %get-tuple-element.139), channel_id=1, source_target_pairs={{0,1},{1,2},{2,3},{3,4},{4,5},{5,6},{6,7},{7,8},{8,9},{9,10},{10,1... | collective-permute-start | bytes 663560 | tf_op jit(solution)/shard_map/ppermute | solution.py:538
  97.0 0.0 collective-permute-start.17
  97.0 2.7 %collective-permute-start.18 = (bf16[162,512]{1,0:T(8,128)(2,1)S(1)}, bf16[162,512]{1,0:T(8,128)(2,1)S(1)}, u32[]{:S(2)}, u32[]{:S(2)}) collective-permute-start(bf16[162,512]{1,0:T(8,128)(2,1)S(1)} %get-tuple-element.135), channel_id=1, source_target_pairs={{0,16},{16,32},{32,48},{48,64},{64,80},{80,96},{96,112},{112,0},{1... | collective-permute-start | bytes 497672 | tf_op jit(solution)/shard_map/ppermute | solution.py:538
  99.7 2.7 %collective-permute-start.19 = (bf16[54,512]{1,0:T(8,128)(2,1)S(1)}, bf16[54,512]{1,0:T(8,128)(2,1)S(1)}, u32[]{:S(2)}, u32[]{:S(2)}) collective-permute-start(bf16[54,512]{1,0:T(8,128)(2,1)S(1)} %get-tuple-element.137), channel_id=1, source_target_pairs={{0,17},{1,18},{2,19},{3,20},{4,21},{5,22},{6,23},{7,24},{8,25},{9,... | collective-permute-start | bytes 165896 | tf_op jit(solution)/shard_map/ppermute | solution.py:548
  102.5 12.1 %all-to-all-done = bf16[64,8,1024]{2,1,0:T(8,128)(2,1)S(1)} async-done(((bf16[64,8,1024]{2,1,0:T(8,128)(2,1)}), bf16[64,8,1024]{2,1,0:T(8,128)(2,1)S(1)}, u32[]{:S(2)}, u32[]{:S(2)}) %all-to-all-start) | async-done | bytes 1048608 | tf_op jit(solution)/shard_map/all_to_all | solution.py:563
  114.6 0.2 convert_reduce_fusion
  114.8 3.7 %collective-permute-done.18.lon_ref = bf16[162,512]{1,0:T(8,128)(2,1)S(1)} collective-permute-done((bf16[162,512]{1,0:T(8,128)(2,1)S(1)}, bf16[162,512]{1,0:T(8,128)(2,1)S(1)}, u32[]{:S(2)}, u32[]{:S(2)}) %collective-permute-start.18) | collective-permute-done | bytes 165920 | tf_op jit(solution)/shard_map/ppermute | solution.py:538
  118.4 1.6 %collective-permute-done.19.corner_ref = bf16[54,512]{1,0:T(8,128)(2,1)S(1)} collective-permute-done((bf16[54,512]{1,0:T(8,128)(2,1)S(1)}, bf16[54,512]{1,0:T(8,128)(2,1)S(1)}, u32[]{:S(2)}, u32[]{:S(2)}) %collective-permute-start.19) | collective-permute-done | bytes 55328 | tf_op jit(solution)/shard_map/ppermute | solution.py:548
  120.1 2.3 %collective-permute-start.20 = (f32[4,1024]{1,0:T(4,128)S(1)}, f32[4,1024]{1,0:T(4,128)S(1)}, u32[]{:S(2)}, u32[]{:S(2)}) collective-permute-start(f32[4,1024]{1,0:T(4,128)S(1)} %slice_select_fusion), channel_id=1, source_target_pairs={{0,1},{1,0},{2,3},{3,2},{4,5},{5,4},{6,7},{7,6},{8,9},{9,8},{10,11... | collective-permute-start | bytes 49160 | tf_op jit(solution)/shard_map/ppermute | solution.py:570
  122.3 1.3 %assemble.1 = bf16[864,512]{1,0:T(8,128)(2,1)} custom-call(bf16[2,216,512]{2,1,0:T(8,128)(2,1)S(1)} %get-tuple-element.131.g0_ref, bf16[2,216,512]{2,1,0:T(8,128)(2,1)S(1)} %get-tuple-element.132.g1_ref, bf16[216,512]{1,0:T(8,128)(2,1)S(1)} %collective-permute-done.17.lat_ref, bf16[162,512]{1,0:T(8,128)(2,1)S(1)} %collective-permute-done.18.lon_ref, ...), custom_call_target="tpu_custom_call" | custom-call | flops 2000000000 | bytes 4194304 | tf_op jit(solution)/shard_map/assemble/pallas_call | solution.py:429
  123.6 1.2 maximum_bitcast_fusion
  124.8 0.6 pad_maximum_fusion.3
  (39 shorter events, 0.1 us)
Async XLA Ops:
  0.6 1.2 copy-start.2
  1.8 10.9 %copy-start.1 = (bf16[512,2048]{1,0:T(8,128)(2,1)S(1)}, bf16[512,2048]{1,0:T(8,128)(2,1)}, u32[]{:S(2)}) copy-start(bf16[512,2048]{1,0:T(8,128)(2,1)} %w_ref.3) | copy-start | bytes 6291460
  1.9 11.3 %collective-permute-start = (bf16[216,512]{1,0:T(8,128)(2,1)S(1)}, bf16[216,512]{1,0:T(8,128)(2,1)S(1)}, u32[]{:S(2)}, u32[]{:S(2)}) collective-permute-start(bf16[216,512]{1,0:T(8,128)(2,1)S(1)} %get-tuple-element.71), channel_id=1, source_target_pairs={{0,15},{1,0},{2,1},{3,2},{4,3},{5,4},{6,5},{7,6},{8,7},{9,8},{10,9... | collective-permute-start | bytes 663560 | tf_op jit(solution)/shard_map/ppermute | solution.py:538
  3.4 24.7 %collective-permute-start.1 = (bf16[162,512]{1,0:T(8,128)(2,1)S(1)}, bf16[162,512]{1,0:T(8,128)(2,1)S(1)}, u32[]{:S(2)}, u32[]{:S(2)}) collective-permute-start(bf16[162,512]{1,0:T(8,128)(2,1)S(1)} %get-tuple-element.73), channel_id=1, source_target_pairs={{0,112},{16,0},{32,16},{48,32},{64,48},{80,64},{96,80},{112,96},{1... | collective-permute-start | bytes 497672 | tf_op jit(solution)/shard_map/ppermute | solution.py:538
  9.5 18.5 %collective-permute-start.2 = (bf16[54,512]{1,0:T(8,128)(2,1)S(1)}, bf16[54,512]{1,0:T(8,128)(2,1)S(1)}, u32[]{:S(2)}, u32[]{:S(2)}) collective-permute-start(bf16[54,512]{1,0:T(8,128)(2,1)S(1)} %get-tuple-element.74), channel_id=1, source_target_pairs={{0,127},{1,112},{2,113},{3,114},{4,115},{5,116},{6,117},{7,118},{8... | collective-permute-start | bytes 165896 | tf_op jit(solution)/shard_map/ppermute | solution.py:548
  12.7 1.1 copy-start.12
  12.7 4.7 %copy-start.3 = (bf16[24,12,3,512]{3,0,2,1:T(8,128)(2,1)S(1)}, bf16[24,12,3,512]{3,0,2,1:T(8,128)(2,1)}, u32[]{:S(2)}) copy-start(bf16[24,12,3,512]{3,0,2,1:T(8,128)(2,1)} %param.11) | copy-start | bytes 2654212
  12.7 4.7 %copy-start.7 = (f32[512]{0:T(512)S(1)}, f32[512]{0:T(512)}, u32[]{:S(2)}) copy-start(f32[512]{0:T(512)} %param.13) | copy-start | bytes 6148
  12.7 4.7 %copy-start.9 = (f32[8]{0:T(128)S(1)}, f32[8]{0:T(128)}, u32[]{:S(2)}) copy-start(f32[8]{0:T(128)} %refs_11_.3) | copy-start | bytes 100
  14.0 10.7 %collective-permute-start.5 = (bf16[6,3,6,1024]{3,1,0,2:T(4,128)(2,1)S(1)}, bf16[6,3,6,1024]{3,1,0,2:T(4,128)(2,1)S(1)}, u32[]{:S(2)}, u32[]{:S(2)}) collective-permute-start(bf16[6,3,6,1024]{3,1,0,2:T(4,128)(2,1)S(1)} %get-tuple-element.146), channel_id=1, source_target_pairs={{0,112},{16,0},{32,16},{48,32},{64,48},{80,64},{96,80},{112,96},{1... | collective-permute-start | bytes 663560 | tf_op jit(solution)/shard_map/ppermute | solution.py:538
  21.9 11.2 %collective-permute-start.3 = (bf16[162,512]{1,0:T(8,128)(2,1)S(1)}, bf16[162,512]{1,0:T(8,128)(2,1)S(1)}, u32[]{:S(2)}, u32[]{:S(2)}) collective-permute-start(bf16[162,512]{1,0:T(8,128)(2,1)S(1)} %get-tuple-element.78), channel_id=1, source_target_pairs={{0,112},{16,0},{32,16},{48,32},{64,48},{80,64},{96,80},{112,96},{1... | collective-permute-start | bytes 497672 | tf_op jit(solution)/shard_map/ppermute | solution.py:538
  22.0 11.1 %collective-permute-start.4 = (bf16[54,512]{1,0:T(8,128)(2,1)S(1)}, bf16[54,512]{1,0:T(8,128)(2,1)S(1)}, u32[]{:S(2)}, u32[]{:S(2)}) collective-permute-start(bf16[54,512]{1,0:T(8,128)(2,1)S(1)} %get-tuple-element.79), channel_id=1, source_target_pairs={{0,127},{1,112},{2,113},{3,114},{4,115},{5,116},{6,117},{7,118},{8... | collective-permute-start | bytes 165896 | tf_op jit(solution)/shard_map/ppermute | solution.py:548
  25.0 18.1 %slice-start = ((s8[8388608]{0:T(1024)(128)(4,1)}), s8[4194304]{0:T(1024)(128)(4,1)S(1)}, s32[]{:S(2)}) async-start(s8[8388608]{0:T(1024)(128)(4,1)} %bitcast.21), calls=%async_computation.1 | async-start | bytes 8388608
  25.3 7.1 %collective-permute-start.6 = (bf16[3,3,12,1024]{3,1,0,2:T(4,128)(2,1)S(1)}, bf16[3,3,12,1024]{3,1,0,2:T(4,128)(2,1)S(1)}, u32[]{:S(2)}, u32[]{:S(2)}) collective-permute-start(bf16[3,3,12,1024]{3,1,0,2:T(4,128)(2,1)S(1)} %get-tuple-element.144), channel_id=1, source_target_pairs={{0,15},{1,0},{2,1},{3,2},{4,3},{5,4},{6,5},{7,6},{8,7},{9,8},{10,9... | collective-permute-start | bytes 663560 | tf_op jit(solution)/shard_map/ppermute | solution.py:538
  28.0 15.1 %slice-start.1 = ((s8[8388608]{0:T(1024)(128)(4,1)}), s8[4194304]{0:T(1024)(128)(4,1)S(1)}, s32[]{:S(2)}) async-start(s8[8388608]{0:T(1024)(128)(4,1)} %bitcast.21), calls=%async_computation.2 | async-start | bytes 8388608
  32.3 1.2 copy-start.4
  33.1 10.1 %collective-permute-start.7 = (bf16[224,512]{1,0:T(8,128)(2,1)S(1)}, bf16[224,512]{1,0:T(8,128)(2,1)S(1)}, u32[]{:S(2)}, u32[]{:S(2)}) collective-permute-start(bf16[224,512]{1,0:T(8,128)(2,1)S(1)} %get-tuple-element.82), channel_id=1, source_target_pairs={{0,15},{1,0},{2,1},{3,2},{4,3},{5,4},{6,5},{7,6},{8,7},{9,8},{10,9... | collective-permute-start | bytes 688136 | tf_op jit(solution)/shard_map/ppermute | solution.py:538
  33.5 9.7 %copy-start = (bf16[2048,1024]{1,0:T(8,128)(2,1)S(1)}, bf16[2048,1024]{1,0:T(8,128)(2,1)}, u32[]{:S(2)}) copy-start(bf16[2048,1024]{1,0:T(8,128)(2,1)} %mw_ref.1) | copy-start | bytes 12582916
  33.5 9.7 %copy-start.5 = (f32[2048]{0:T(1024)S(1)}, f32[2048]{0:T(1024)}, u32[]{:S(2)}) copy-start(f32[2048]{0:T(1024)} %param.15) | copy-start | bytes 24580
  33.5 9.7 %copy-start.6 = (f32[1024]{0:T(1024)S(1)}, f32[1024]{0:T(1024)}, u32[]{:S(2)}) copy-start(f32[1024]{0:T(1024)} %param.18) | copy-start | bytes 12292
  33.5 9.7 %copy-start.8 = (f32[16]{0:T(128)S(1)}, f32[16]{0:T(128)}, u32[]{:S(2)}) copy-start(f32[16]{0:T(128)} %scale_ref.1) | copy-start | bytes 196
  33.6 23.8 %collective-permute-start.8 = (bf16[216,512]{1,0:T(8,128)(2,1)S(1)}, bf16[216,512]{1,0:T(8,128)(2,1)S(1)}, u32[]{:S(2)}, u32[]{:S(2)}) collective-permute-start(bf16[216,512]{1,0:T(8,128)(2,1)S(1)} %get-tuple-element.93), channel_id=1, source_target_pairs={{0,15},{1,0},{2,1},{3,2},{4,3},{5,4},{6,5},{7,6},{8,7},{9,8},{10,9... | collective-permute-start | bytes 663560 | tf_op jit(solution)/shard_map/ppermute | solution.py:538
  37.3 20.1 %collective-permute-start.9 = (bf16[162,512]{1,0:T(8,128)(2,1)S(1)}, bf16[162,512]{1,0:T(8,128)(2,1)S(1)}, u32[]{:S(2)}, u32[]{:S(2)}) collective-permute-start(bf16[162,512]{1,0:T(8,128)(2,1)S(1)} %get-tuple-element.94), channel_id=1, source_target_pairs={{0,112},{16,0},{32,16},{48,32},{64,48},{80,64},{96,80},{112,96},{1... | collective-permute-start | bytes 497672 | tf_op jit(solution)/shard_map/ppermute | solution.py:538
  43.0 14.5 %collective-permute-start.10 = (bf16[54,512]{1,0:T(8,128)(2,1)S(1)}, bf16[54,512]{1,0:T(8,128)(2,1)S(1)}, u32[]{:S(2)}, u32[]{:S(2)}) collective-permute-start(bf16[54,512]{1,0:T(8,128)(2,1)S(1)} %get-tuple-element.95), channel_id=1, source_target_pairs={{0,127},{1,112},{2,113},{3,114},{4,115},{5,116},{6,117},{7,118},{8... | collective-permute-start | bytes 165896 | tf_op jit(solution)/shard_map/ppermute | solution.py:548
  57.4 6.0 %collective-permute-start.11 = (bf16[216,512]{1,0:T(8,128)(2,1)S(1)}, bf16[216,512]{1,0:T(8,128)(2,1)S(1)}, u32[]{:S(2)}, u32[]{:S(2)}) collective-permute-start(bf16[216,512]{1,0:T(8,128)(2,1)S(1)} %get-tuple-element.96), channel_id=1, source_target_pairs={{0,1},{1,2},{2,3},{3,4},{4,5},{5,6},{6,7},{7,8},{8,9},{9,10},{10,1... | collective-permute-start | bytes 663560 | tf_op jit(solution)/shard_map/ppermute | solution.py:538
  58.8 17.3 %collective-permute-start.14 = (bf16[162,512]{1,0:T(8,128)(2,1)S(1)}, bf16[162,512]{1,0:T(8,128)(2,1)S(1)}, u32[]{:S(2)}, u32[]{:S(2)}) collective-permute-start(bf16[162,512]{1,0:T(8,128)(2,1)S(1)} %get-tuple-element.113), channel_id=1, source_target_pairs={{0,16},{16,32},{32,48},{48,64},{64,80},{80,96},{96,112},{112,0},{1... | collective-permute-start | bytes 497672 | tf_op jit(solution)/shard_map/ppermute | solution.py:538
  61.7 14.3 %collective-permute-start.15 = (bf16[54,512]{1,0:T(8,128)(2,1)S(1)}, bf16[54,512]{1,0:T(8,128)(2,1)S(1)}, u32[]{:S(2)}, u32[]{:S(2)}) collective-permute-start(bf16[54,512]{1,0:T(8,128)(2,1)S(1)} %get-tuple-element.114), channel_id=1, source_target_pairs={{0,17},{1,18},{2,19},{3,20},{4,21},{5,22},{6,23},{7,24},{8,25},{9,... | collective-permute-start | bytes 165896 | tf_op jit(solution)/shard_map/ppermute | solution.py:548
  63.7 11.1 %collective-permute-start.12 = (bf16[6,3,6,1024]{3,1,0,2:T(4,128)(2,1)S(1)}, bf16[6,3,6,1024]{3,1,0,2:T(4,128)(2,1)S(1)}, u32[]{:S(2)}, u32[]{:S(2)}) collective-permute-start(bf16[6,3,6,1024]{3,1,0,2:T(4,128)(2,1)S(1)} %copy.17), channel_id=1, source_target_pairs={{0,16},{16,32},{32,48},{48,64},{64,80},{80,96},{96,112},{112,0},{1... | collective-permute-start | bytes 663560 | tf_op jit(solution)/shard_map/ppermute | solution.py:538
  82.6 5.6 %collective-permute-start.16 = (bf16[512,1024]{1,0:T(8,128)(2,1)S(1)}, bf16[512,1024]{1,0:T(8,128)(2,1)S(1)}, u32[]{:S(2)}, u32[]{:S(2)}) collective-permute-start(bf16[512,1024]{1,0:T(8,128)(2,1)S(1)} %get-tuple-element.123), channel_id=1, source_target_pairs={{0,1},{1,0},{2,3},{3,2},{4,5},{5,4},{6,7},{7,6},{8,9},{9,8},{10,11... | collective-permute-start | bytes 3145736 | tf_op jit(solution)/shard_map/ppermute | solution.py:615
  88.3 6.2 %copy-start.10 = (bf16[6,3,12,1024]{3,1,0,2:T(4,128)(2,1)S(1)}, bf16[6,3,12,1024]{3,1,0,2:T(4,128)(2,1)}, u32[]{:S(2)}) copy-start(bf16[6,3,12,1024]{3,1,0,2:T(4,128)(2,1)} %pad_maximum_fusion.2) | copy-start | bytes 1327108
  89.7 24.9 %all-to-all-start = ((bf16[64,8,1024]{2,1,0:T(8,128)(2,1)}), bf16[64,8,1024]{2,1,0:T(8,128)(2,1)S(1)}, u32[]{:S(2)}, u32[]{:S(2)}) async-start(bf16[64,8,1024]{2,1,0:T(8,128)(2,1)} %fusion), calls=%async_computation | async-start | bytes 2097152 | tf_op jit(solution)/shard_map/all_to_all | solution.py:563
  95.5 19.2 %collective-permute-start.13 = (bf16[3,3,12,1024]{3,1,0,2:T(4,128)(2,1)}, bf16[3,3,12,1024]{3,1,0,2:T(4,128)(2,1)S(1)}, u32[]{:S(2)}, u32[]{:S(2)}) collective-permute-start(bf16[3,3,12,1024]{3,1,0,2:T(4,128)(2,1)} %get-tuple-element.139), channel_id=1, source_target_pairs={{0,1},{1,2},{2,3},{3,4},{4,5},{5,6},{6,7},{7,8},{8,9},{9,10},{10,1... | collective-permute-start | bytes 663560 | tf_op jit(solution)/shard_map/ppermute | solution.py:538
  97.0 17.8 %collective-permute-start.17 = (bf16[216,512]{1,0:T(8,128)(2,1)S(1)}, bf16[216,512]{1,0:T(8,128)(2,1)S(1)}, u32[]{:S(2)}, u32[]{:S(2)}) collective-permute-start(bf16[216,512]{1,0:T(8,128)(2,1)S(1)} %get-tuple-element.133), channel_id=1, source_target_pairs={{0,1},{1,2},{2,3},{3,4},{4,5},{5,6},{6,7},{7,8},{8,9},{9,10},{10,1... | collective-permute-start | bytes 663560 | tf_op jit(solution)/shard_map/ppermute | solution.py:538
  97.0 21.4 %collective-permute-start.18 = (bf16[162,512]{1,0:T(8,128)(2,1)S(1)}, bf16[162,512]{1,0:T(8,128)(2,1)S(1)}, u32[]{:S(2)}, u32[]{:S(2)}) collective-permute-start(bf16[162,512]{1,0:T(8,128)(2,1)S(1)} %get-tuple-element.135), channel_id=1, source_target_pairs={{0,16},{16,32},{32,48},{48,64},{64,80},{80,96},{96,112},{112,0},{1... | collective-permute-start | bytes 497672 | tf_op jit(solution)/shard_map/ppermute | solution.py:538
  99.7 20.3 %collective-permute-start.19 = (bf16[54,512]{1,0:T(8,128)(2,1)S(1)}, bf16[54,512]{1,0:T(8,128)(2,1)S(1)}, u32[]{:S(2)}, u32[]{:S(2)}) collective-permute-start(bf16[54,512]{1,0:T(8,128)(2,1)S(1)} %get-tuple-element.137), channel_id=1, source_target_pairs={{0,17},{1,18},{2,19},{3,20},{4,21},{5,22},{6,23},{7,24},{8,25},{9,... | collective-permute-start | bytes 165896 | tf_op jit(solution)/shard_map/ppermute | solution.py:548
  120.1 4.8 %collective-permute-start.20 = (f32[4,1024]{1,0:T(4,128)S(1)}, f32[4,1024]{1,0:T(4,128)S(1)}, u32[]{:S(2)}, u32[]{:S(2)}) collective-permute-start(f32[4,1024]{1,0:T(4,128)S(1)} %slice_select_fusion), channel_id=1, source_target_pairs={{0,1},{1,0},{2,3},{3,2},{4,5},{5,4},{6,7},{7,6},{8,9},{9,8},{10,11... | collective-permute-start | bytes 49160 | tf_op jit(solution)/shard_map/ppermute | solution.py:570
  122.3 1.3 %copy-start.11 = (bf16[3,3,12,1024]{3,1,0,2:T(4,128)(2,1)S(1)}, bf16[3,3,12,1024]{3,1,0,2:T(4,128)(2,1)}, u32[]{:S(2)}) copy-start(bf16[3,3,12,1024]{3,1,0,2:T(4,128)(2,1)} %get-tuple-element.140) | copy-start | bytes 663556

commit v2 on v1

--- a/solution.py
+++ b/solution.py
@@ -206,8 +206,8 @@
         for win in range(2):
             near[cut, TOK * win : TOK * win + TOK, :] = y0_ref[win, :, lanes].astype(F32)
             far[cut, TOK * win : TOK * win + TOK, :] = y1_ref[win, :, lanes].astype(F32)
-        near[cut, 2 * TOK :, :] = lat_ref[0:112, lanes].astype(F32)
-        far[cut, 2 * TOK :, :] = lat_ref[112:224, lanes].astype(F32)
+        near[cut, 2 * TOK : 2 * TOK + 112, :] = lat_ref[0:112, lanes].astype(F32)
+        far[cut, 2 * TOK : 2 * TOK + 112, :] = lat_ref[112:224, lanes].astype(F32)
         halo[cut, 0:162, :] = lon_ref[:, lanes].astype(F32)
         halo[cut, 162:TOK, :] = corner_ref[:, lanes].astype(F32)
     for group in range(18):
@@ -275,7 +275,7 @@
                     WIN * group : WIN * group + WIN,
                     part * D1 + cut * 128 : part * D1 + cut * 128 + 128,
                 ]
-    done = jnp.concatenate([cells[cut] for cut in range(4)], -1)
+    done = jnp.concatenate([cells[cut, 0:GROUPS] for cut in range(4)], -1)
     g_ref[...] = done.reshape(ROWS, D1).astype(BF16)
     glat_ref[...] = done[GROUPS - EDGE :].reshape(EDGE * LON, D1).astype(BF16)
     for group in range(GROUPS):
@@ -476,10 +476,10 @@
 def coarse_both(ins, cot_coarse, mgain, mw, cw, gain, scales, last):
     outs = [((D2, TOK), BF16), ((TOK, D2), BF16), ((ROWS, D1), BF16), LAT_BLOCK, LON_BLOCK, CORNER]
     scratch = [
-        ((4, 2 * TOK + 112, 128), F32),
-        ((4, 2 * TOK + 112, 128), F32),
-        ((4, TOK, 128), F32),
-        ((4, GROUPS, LON, 128), F32),
+        ((4, 2 * TOK + 128, 128), F32),
+        ((4, 2 * TOK + 128, 128), F32),
+        ((4, TOK + 16, 128), F32),
+        ((4, GROUPS + 1, LON, 128), F32),
         ((TOK, 4 * D1), F32),
         ((TOK, 4 * D1), F32),
         ((TOK, 128), F32),

time: 126 us -> 126 us (level)
  no operation moved by 1% of the time
where the time goes in v2:
time: 126 us; the launch traced here: 125 us
  starting transfers between devices  52 us (41%)
  Pallas kernels  40.1 us (32%)
  waiting for transfers between devices  22.7 us (18%)
  other arithmetic  5.38 us (4%)
  local copies, waits for them, and re-layouts  4.33 us (3%)
    pallas_call x12, Pallas kernels, call(): pl.pallas_call(kernel, out_shape=[jax.ShapeDtypeStruct(shape, kind) for s...  40.1 us
    ppermute x14, starting transfers between devices, moved(): return lax.ppermute(block, axis, ring(lax.axis_size(axis), step))  33.4 us
    all_to_all x1, waiting for transfers between devices, chip_sum(): pieces = lax.all_to_all(part.reshape(64, 8, 2 * D1), ('lon', 'chip'), 0, 0)  12.1 us
    ppermute x14, waiting for transfers between devices, moved(): return lax.ppermute(block, axis, ring(lax.axis_size(axis), step))  8.9 us
    ppermute x5, starting transfers between devices, moved_both(): return lax.ppermute(block, ('lon', *LAT_AXES), route)  8.79 us
    all_to_all x1, starting transfers between devices, chip_sum(): pieces = lax.all_to_all(part.reshape(64, 8, 2 * D1), ('lon', 'chip'), 0, 0)  4.8 us
    ppermute x1, starting transfers between devices, on_device(): sent = lax.ppermute(send, 'core', [(0, 1), (1, 0)])  2.83 us
  transfers between devices with their start and end apart: 22, of which 4 were waited for; matrix products, arithmetic and copies ran while one was open for 4% of the time, Pallas kernels for 27%

profile of v2, /device:TPU:1, one launch (start us, length us, event | category | flops | bytes accessed | tf_op | source)
XLA Modules:
  0.0 125.5 jit_solution(5840508246090414667)
XLA Ops:
  0.6 0.0 copy-start.2
  0.6 1.2 copy-done.2
  1.8 0.1 edges.2
  1.9 1.5 %collective-permute-start = (bf16[216,512]{1,0:T(8,128)(2,1)S(1)}, bf16[216,512]{1,0:T(8,128)(2,1)S(1)}, u32[]{:S(2)}, u32[]{:S(2)}) collective-permute-start(bf16[216,512]{1,0:T(8,128)(2,1)S(1)} %get-tuple-element.71), channel_id=1, source_target_pairs={{0,15},{1,0},{2,1},{3,2},{4,3},{5,4},{6,5},{7,6},{8,7},{9,8},{10,9... | collective-permute-start | bytes 663560 | tf_op jit(solution)/shard_map/ppermute | solution.py:538
  3.4 6.1 %collective-permute-start.1 = (bf16[162,512]{1,0:T(8,128)(2,1)S(1)}, bf16[162,512]{1,0:T(8,128)(2,1)S(1)}, u32[]{:S(2)}, u32[]{:S(2)}) collective-permute-start(bf16[162,512]{1,0:T(8,128)(2,1)S(1)} %get-tuple-element.73), channel_id=1, source_target_pairs={{0,112},{16,0},{32,16},{48,32},{64,48},{80,64},{96,80},{112,96},{1... | collective-permute-start | bytes 497672 | tf_op jit(solution)/shard_map/ppermute | solution.py:538
  9.5 3.2 %collective-permute-start.2 = (bf16[54,512]{1,0:T(8,128)(2,1)S(1)}, bf16[54,512]{1,0:T(8,128)(2,1)S(1)}, u32[]{:S(2)}, u32[]{:S(2)}) collective-permute-start(bf16[54,512]{1,0:T(8,128)(2,1)S(1)} %get-tuple-element.74), channel_id=1, source_target_pairs={{0,127},{1,112},{2,113},{3,114},{4,115},{5,116},{6,117},{7,118},{8... | collective-permute-start | bytes 165896 | tf_op jit(solution)/shard_map/ppermute | solution.py:548
  12.7 0.0 copy-start.9
  12.7 0.5 turn.1.refs_2_.refs_5_
  13.2 0.0 collective-permute-done.refs_1_
  13.2 0.6 copy-done.12
  13.8 0.2 fusion.4
  14.0 3.5 %collective-permute-start.5 = (bf16[6,3,6,1024]{3,1,0,2:T(4,128)(2,1)S(1)}, bf16[6,3,6,1024]{3,1,0,2:T(4,128)(2,1)S(1)}, u32[]{:S(2)}, u32[]{:S(2)}) collective-permute-start(bf16[6,3,6,1024]{3,1,0,2:T(4,128)(2,1)S(1)} %get-tuple-element.146), channel_id=1, source_target_pairs={{0,112},{16,0},{32,16},{48,32},{64,48},{80,64},{96,80},{112,96},{1... | collective-permute-start | bytes 663560 | tf_op jit(solution)/shard_map/ppermute | solution.py:538
  17.4 4.4 %fine_forward_0.1 = (bf16[2,216,512]{2,1,0:T(8,128)(2,1)S(1)}, bf16[112,512]{1,0:T(8,128)(2,1)S(1)}, bf16[162,512]{1,0:T(8,128)(2,1)S(1)}, bf16[54,512]{1,0:T(8,...) custom-call(bf16[864,512]{1,0:T(8,128)(2,1)S(1)} %bitcast.26, ...), custom_call_target="tpu_custom_call" | custom-call | flops 10000000000 | bytes 4194304 | tf_op jit(solution)/shard_map/fine_forward_0/pallas_call | solution.py:429
  21.9 0.1 collective-permute-start.3
  22.0 2.7 %collective-permute-start.4 = (bf16[54,512]{1,0:T(8,128)(2,1)S(1)}, bf16[54,512]{1,0:T(8,128)(2,1)S(1)}, u32[]{:S(2)}, u32[]{:S(2)}) collective-permute-start(bf16[54,512]{1,0:T(8,128)(2,1)S(1)} %get-tuple-element.79), channel_id=1, source_target_pairs={{0,127},{1,112},{2,113},{3,114},{4,115},{5,116},{6,117},{7,118},{8... | collective-permute-start | bytes 165896 | tf_op jit(solution)/shard_map/ppermute | solution.py:548
  24.7 0.0 collective-permute-done.5
  24.7 0.4 pad_maximum_fusion
  25.0 0.0 slice-start
  25.1 0.2 fusion.3
  25.3 2.8 %collective-permute-start.6 = (bf16[3,3,12,1024]{3,1,0,2:T(4,128)(2,1)S(1)}, bf16[3,3,12,1024]{3,1,0,2:T(4,128)(2,1)S(1)}, u32[]{:S(2)}, u32[]{:S(2)}) collective-permute-start(bf16[3,3,12,1024]{3,1,0,2:T(4,128)(2,1)S(1)} %get-tuple-element.144), channel_id=1, source_target_pairs={{0,15},{1,0},{2,1},{3,2},{4,3},{5,4},{6,5},{7,6},{8,7},{9,8},{10,9... | collective-permute-start | bytes 663560 | tf_op jit(solution)/shard_map/ppermute | solution.py:538
  28.0 4.3 %fine_forward_1.1 = (bf16[2,216,512]{2,1,0:T(8,128)(2,1)S(1)}, bf16[224,512]{1,0:T(8,128)(2,1)S(1)}, bf16[2,216,512]{2,1,0:T(8,128)(2,1)S(1)}, bf16[2,1536,216]{...) custom-call(bf16[864,512]{1,0:T(8,128)(2,1)S(1)} %bitcast.27, ...), custom_call_target="tpu_custom_call" | custom-call | flops 10000000000 | bytes 4194304 | tf_op jit(solution)/shard_map/fine_forward_1/pallas_call | solution.py:429
  32.3 0.0 copy-start.4
  32.3 0.4 pad_maximum_fusion.1
  32.7 0.3 copy.14
  33.1 0.0 collective-permute-done.4.corner_ref
  33.1 0.0 collective-permute-done.3.lon_ref
  33.1 0.1 collective-permute-start.7
  33.2 0.3 copy-done.4
  33.5 0.1 edges.3
  33.6 3.7 %collective-permute-start.8 = (bf16[216,512]{1,0:T(8,128)(2,1)S(1)}, bf16[216,512]{1,0:T(8,128)(2,1)S(1)}, u32[]{:S(2)}, u32[]{:S(2)}) collective-permute-start(bf16[216,512]{1,0:T(8,128)(2,1)S(1)} %get-tuple-element.93), channel_id=1, source_target_pairs={{0,15},{1,0},{2,1},{3,2},{4,3},{5,4},{6,5},{7,6},{8,7},{9,8},{10,9... | collective-permute-start | bytes 663560 | tf_op jit(solution)/shard_map/ppermute | solution.py:538
  37.3 5.7 %collective-permute-start.9 = (bf16[162,512]{1,0:T(8,128)(2,1)S(1)}, bf16[162,512]{1,0:T(8,128)(2,1)S(1)}, u32[]{:S(2)}, u32[]{:S(2)}) collective-permute-start(bf16[162,512]{1,0:T(8,128)(2,1)S(1)} %get-tuple-element.94), channel_id=1, source_target_pairs={{0,112},{16,0},{32,16},{48,32},{64,48},{80,64},{96,80},{112,96},{1... | collective-permute-start | bytes 497672 | tf_op jit(solution)/shard_map/ppermute | solution.py:538
  43.0 0.2 collective-permute-start.10
  43.2 14.2 %coarse_both.1 = (bf16[1024,216]{1,0:T(8,128)(2,1)S(1)}, bf16[216,1024]{1,0:T(8,128)(2,1)S(1)}, bf16[864,512]{1,0:T(8,128)(2,1)S(1)}, bf16[216,512]{1,0:T(8,128)...) custom-call(bf16[2,216,512]{2,1,0:T(8,128)(2,1)S(1)} %get-tuple-element.72.y0_ref, ...), custom_call_target="tpu_custom_call" | custom-call | flops 20000000000 | bytes 4194304 | tf_op jit(solution)/shard_map/coarse_both/pallas_call | solution.py:429
  57.4 0.0 collective-permute-done.10.refs_5_
  57.5 1.3 %collective-permute-start.11 = (bf16[216,512]{1,0:T(8,128)(2,1)S(1)}, bf16[216,512]{1,0:T(8,128)(2,1)S(1)}, u32[]{:S(2)}, u32[]{:S(2)}) collective-permute-start(bf16[216,512]{1,0:T(8,128)(2,1)S(1)} %get-tuple-element.96), channel_id=1, source_target_pairs={{0,1},{1,2},{2,3},{3,4},{4,5},{5,6},{6,7},{7,8},{8,9},{9,10},{10,1... | collective-permute-start | bytes 663560 | tf_op jit(solution)/shard_map/ppermute | solution.py:538
  58.7 3.0 %collective-permute-start.14 = (bf16[162,512]{1,0:T(8,128)(2,1)S(1)}, bf16[162,512]{1,0:T(8,128)(2,1)S(1)}, u32[]{:S(2)}, u32[]{:S(2)}) collective-permute-start(bf16[162,512]{1,0:T(8,128)(2,1)S(1)} %get-tuple-element.113), channel_id=1, source_target_pairs={{0,16},{16,32},{32,48},{48,64},{64,80},{80,96},{96,112},{112,0},{1... | collective-permute-start | bytes 497672 | tf_op jit(solution)/shard_map/ppermute | solution.py:538
  61.7 0.7 coarse_out.1
  62.5 0.9 normed.1
  63.4 0.1 fusion.2
  63.5 0.2 copy.17
  63.7 1.5 %collective-permute-start.12 = (bf16[6,3,6,1024]{3,1,0,2:T(4,128)(2,1)S(1)}, bf16[6,3,6,1024]{3,1,0,2:T(4,128)(2,1)S(1)}, u32[]{:S(2)}, u32[]{:S(2)}) collective-permute-start(bf16[6,3,6,1024]{3,1,0,2:T(4,128)(2,1)S(1)} %copy.17), channel_id=1, source_target_pairs={{0,16},{16,32},{32,48},{48,64},{64,80},{80,96},{96,112},{112,0},{1... | collective-permute-start | bytes 663560 | tf_op jit(solution)/shard_map/ppermute | solution.py:538
  65.2 4.2 %fine_backward_1.1 = (bf16[2,1536,256]{2,1,0:T(8,128)(2,1)S(1)}, bf16[2,216,512]{2,1,0:T(8,128)(2,1)S(1)}) custom-call(bf16[864,512]{1,0:T(8,128)(2,1)S(1)} %get-tuple-element.86.refs_0_, bf16[216,512]{1,0:T(8,128)(2,1)S(1)} %collective-permute-done.11.refs_1_, bf16[864,512]{1,0:T(8,128)(2,1)S(1)} %bitcast.29, ...), custom_call_target="tpu_custom_call" | custom-call | flops 10000000000 | bytes 4194304 | tf_op jit(solution)/shard_map/fine_backward_1/pallas_call | solution.py:429
  69.4 0.2 copy.18
  69.6 5.2 %collective-permute-done.12 = bf16[6,3,6,1024]{3,1,0,2:T(4,128)(2,1)S(1)} collective-permute-done((bf16[6,3,6,1024]{3,1,0,2:T(4,128)(2,1)S(1)}, bf16[6,3,6,1024]{3,1,0,2:T(4,128)(2,1)S(1)}, u32[]{:S(2)}, u32[]{:S(2)}) %collective-permute-start.12) | collective-permute-done | bytes 221216 | tf_op jit(solution)/shard_map/ppermute | solution.py:538
  74.8 1.2 pad_maximum_fusion.2
  76.0 6.6 %fine_backward_0.1 = (bf16[2,1536,256]{2,1,0:T(8,128)(2,1)S(1)}, bf16[2,216,512]{2,1,0:T(8,128)(2,1)S(1)}, bf16[512,1024]{1,0:T(8,128)(2,1)S(1)}, bf16[512,1024]{1,0:T(8,128)(2,1)S(1)}) custom-call(bf16[864,512]{1,0:T(8,128)(2,1)S(1)} %get-tuple-element.86.refs_0_, bf16[216,512]{1,0:T(8,128)(2,1)S(1)} %collective-permute-done.11.refs_1_, ...), custom_call_target="tpu_custom_call" | custom-call | flops 10000000000 | bytes 4194304 | tf_op jit(solution)/shard_map/fine_backward_0/pallas_call | solution.py:429
  82.6 2.8 %collective-permute-start.16 = (bf16[512,1024]{1,0:T(8,128)(2,1)S(1)}, bf16[512,1024]{1,0:T(8,128)(2,1)S(1)}, u32[]{:S(2)}, u32[]{:S(2)}) collective-permute-start(bf16[512,1024]{1,0:T(8,128)(2,1)S(1)} %get-tuple-element.123), channel_id=1, source_target_pairs={{0,1},{1,0},{2,3},{3,2},{4,5},{5,4},{6,7},{7,6},{8,9},{9,8},{10,11... | collective-permute-start | bytes 3145736 | tf_op jit(solution)/shard_map/ppermute | solution.py:615
  85.5 2.8 %fine_input.1 = (bf16[2,216,512]{2,1,0:T(8,128)(2,1)S(1)}, bf16[2,216,512]{2,1,0:T(8,128)(2,1)S(1)}, bf16[216,512]{1,0:T(8,128)(2,1)S(1)}, bf16[162,512]{1,0:T(8,128)(2,1)S(1)}, bf16[54,512]{1,0:T(8,128)(2,1)S(1)}) custom-call(bf16[2,1536,256]{2,1,0:T(8,128)(2,1)S(1)} %get-tuple-element.125.gq0_ref, ...), custom_call_target="tpu_custom_call" | custom-call | flops 6000000000 | bytes 4194304 | tf_op jit(solution)/shard_map/fine_input/pallas_call | solution.py:429
  88.3 0.0 copy-start.10
  88.3 1.4 %fusion = bf16[64,8,1024]{2,1,0:T(8,128)(2,1)} fusion(bf16[512,1024]{1,0:T(8,128)(2,1)S(1)} %collective-permute-done.16, bf16[512,1024]{1,0:T(8,128)(2,1)S(1)} %get-tuple-element.128), kind=kLoop, calls=%fused_computation.2 | loop fusion | flops 2097152 | bytes 3145728 | tf_op jit(solution)/shard_map/reshape | solution.py:563
  89.7 4.8 %all-to-all-start = ((bf16[64,8,1024]{2,1,0:T(8,128)(2,1)}), bf16[64,8,1024]{2,1,0:T(8,128)(2,1)S(1)}, u32[]{:S(2)}, u32[]{:S(2)}) async-start(bf16[64,8,1024]{2,1,0:T(8,128)(2,1)} %fusion), calls=%async_computation | async-start | bytes 2097152 | tf_op jit(solution)/shard_map/all_to_all | solution.py:563
  94.5 1.0 fusion.1
  95.5 1.5 %collective-permute-start.13 = (bf16[3,3,12,1024]{3,1,0,2:T(4,128)(2,1)}, bf16[3,3,12,1024]{3,1,0,2:T(4,128)(2,1)S(1)}, u32[]{:S(2)}, u32[]{:S(2)}) collective-permute-start(bf16[3,3,12,1024]{3,1,0,2:T(4,128)(2,1)} %get-tuple-element.139), channel_id=1, source_target_pairs={{0,1},{1,2},{2,3},{3,4},{4,5},{5,6},{6,7},{7,8},{8,9},{9,10},{10,1... | collective-permute-start | bytes 663560 | tf_op jit(solution)/shard_map/ppermute | solution.py:538
  97.0 0.0 collective-permute-start.17
  97.0 2.7 %collective-permute-start.18 = (bf16[162,512]{1,0:T(8,128)(2,1)S(1)}, bf16[162,512]{1,0:T(8,128)(2,1)S(1)}, u32[]{:S(2)}, u32[]{:S(2)}) collective-permute-start(bf16[162,512]{1,0:T(8,128)(2,1)S(1)} %get-tuple-element.135), channel_id=1, source_target_pairs={{0,16},{16,32},{32,48},{48,64},{64,80},{80,96},{96,112},{112,0},{1... | collective-permute-start | bytes 497672 | tf_op jit(solution)/shard_map/ppermute | solution.py:538
  99.7 2.7 %collective-permute-start.19 = (bf16[54,512]{1,0:T(8,128)(2,1)S(1)}, bf16[54,512]{1,0:T(8,128)(2,1)S(1)}, u32[]{:S(2)}, u32[]{:S(2)}) collective-permute-start(bf16[54,512]{1,0:T(8,128)(2,1)S(1)} %get-tuple-element.137), channel_id=1, source_target_pairs={{0,17},{1,18},{2,19},{3,20},{4,21},{5,22},{6,23},{7,24},{8,25},{9,... | collective-permute-start | bytes 165896 | tf_op jit(solution)/shard_map/ppermute | solution.py:548
  102.5 12.1 %all-to-all-done = bf16[64,8,1024]{2,1,0:T(8,128)(2,1)S(1)} async-done(((bf16[64,8,1024]{2,1,0:T(8,128)(2,1)}), bf16[64,8,1024]{2,1,0:T(8,128)(2,1)S(1)}, u32[]{:S(2)}, u32[]{:S(2)}) %all-to-all-start) | async-done | bytes 1048608 | tf_op jit(solution)/shard_map/all_to_all | solution.py:563
  114.6 0.2 convert_reduce_fusion
  114.8 3.7 %collective-permute-done.18.lon_ref = bf16[162,512]{1,0:T(8,128)(2,1)S(1)} collective-permute-done((bf16[162,512]{1,0:T(8,128)(2,1)S(1)}, bf16[162,512]{1,0:T(8,128)(2,1)S(1)}, u32[]{:S(2)}, u32[]{:S(2)}) %collective-permute-start.18) | collective-permute-done | bytes 165920 | tf_op jit(solution)/shard_map/ppermute | solution.py:538
  118.4 1.6 %collective-permute-done.19.corner_ref = bf16[54,512]{1,0:T(8,128)(2,1)S(1)} collective-permute-done((bf16[54,512]{1,0:T(8,128)(2,1)S(1)}, bf16[54,512]{1,0:T(8,128)(2,1)S(1)}, u32[]{:S(2)}, u32[]{:S(2)}) %collective-permute-start.19) | collective-permute-done | bytes 55328 | tf_op jit(solution)/shard_map/ppermute | solution.py:548
  120.1 2.3 %collective-permute-start.20 = (f32[4,1024]{1,0:T(4,128)S(1)}, f32[4,1024]{1,0:T(4,128)S(1)}, u32[]{:S(2)}, u32[]{:S(2)}) collective-permute-start(f32[4,1024]{1,0:T(4,128)S(1)} %slice_select_fusion), channel_id=1, source_target_pairs={{0,1},{1,0},{2,3},{3,2},{4,5},{5,4},{6,7},{7,6},{8,9},{9,8},{10,11... | collective-permute-start | bytes 49160 | tf_op jit(solution)/shard_map/ppermute | solution.py:570
  122.3 1.3 %assemble.1 = bf16[864,512]{1,0:T(8,128)(2,1)} custom-call(bf16[2,216,512]{2,1,0:T(8,128)(2,1)S(1)} %get-tuple-element.131.g0_ref, bf16[2,216,512]{2,1,0:T(8,128)(2,1)S(1)} %get-tuple-element.132.g1_ref, bf16[216,512]{1,0:T(8,128)(2,1)S(1)} %collective-permute-done.17.lat_ref, bf16[162,512]{1,0:T(8,128)(2,1)S(1)} %collective-permute-done.18.lon_ref, ...), custom_call_target="tpu_custom_call" | custom-call | flops 2000000000 | bytes 4194304 | tf_op jit(solution)/shard_map/assemble/pallas_call | solution.py:429
  123.6 1.2 maximum_bitcast_fusion
  124.8 0.6 pad_maximum_fusion.3
  (39 shorter events, 0.1 us)
Async XLA Ops:
  0.6 1.2 copy-start.2
  1.8 10.9 %copy-start.1 = (bf16[512,2048]{1,0:T(8,128)(2,1)S(1)}, bf16[512,2048]{1,0:T(8,128)(2,1)}, u32[]{:S(2)}) copy-start(bf16[512,2048]{1,0:T(8,128)(2,1)} %w_ref.3) | copy-start | bytes 6291460
  1.9 11.3 %collective-permute-start = (bf16[216,512]{1,0:T(8,128)(2,1)S(1)}, bf16[216,512]{1,0:T(8,128)(2,1)S(1)}, u32[]{:S(2)}, u32[]{:S(2)}) collective-permute-start(bf16[216,512]{1,0:T(8,128)(2,1)S(1)} %get-tuple-element.71), channel_id=1, source_target_pairs={{0,15},{1,0},{2,1},{3,2},{4,3},{5,4},{6,5},{7,6},{8,7},{9,8},{10,9... | collective-permute-start | bytes 663560 | tf_op jit(solution)/shard_map/ppermute | solution.py:538
  3.4 24.7 %collective-permute-start.1 = (bf16[162,512]{1,0:T(8,128)(2,1)S(1)}, bf16[162,512]{1,0:T(8,128)(2,1)S(1)}, u32[]{:S(2)}, u32[]{:S(2)}) collective-permute-start(bf16[162,512]{1,0:T(8,128)(2,1)S(1)} %get-tuple-element.73), channel_id=1, source_target_pairs={{0,112},{16,0},{32,16},{48,32},{64,48},{80,64},{96,80},{112,96},{1... | collective-permute-start | bytes 497672 | tf_op jit(solution)/shard_map/ppermute | solution.py:538
  9.5 18.5 %collective-permute-start.2 = (bf16[54,512]{1,0:T(8,128)(2,1)S(1)}, bf16[54,512]{1,0:T(8,128)(2,1)S(1)}, u32[]{:S(2)}, u32[]{:S(2)}) collective-permute-start(bf16[54,512]{1,0:T(8,128)(2,1)S(1)} %get-tuple-element.74), channel_id=1, source_target_pairs={{0,127},{1,112},{2,113},{3,114},{4,115},{5,116},{6,117},{7,118},{8... | collective-permute-start | bytes 165896 | tf_op jit(solution)/shard_map/ppermute | solution.py:548
  12.7 1.1 copy-start.12
  12.7 4.7 %copy-start.3 = (bf16[24,12,3,512]{3,0,2,1:T(8,128)(2,1)S(1)}, bf16[24,12,3,512]{3,0,2,1:T(8,128)(2,1)}, u32[]{:S(2)}) copy-start(bf16[24,12,3,512]{3,0,2,1:T(8,128)(2,1)} %param.11) | copy-start | bytes 2654212
  12.7 4.7 %copy-start.7 = (f32[512]{0:T(512)S(1)}, f32[512]{0:T(512)}, u32[]{:S(2)}) copy-start(f32[512]{0:T(512)} %param.13) | copy-start | bytes 6148
  12.7 4.7 %copy-start.9 = (f32[8]{0:T(128)S(1)}, f32[8]{0:T(128)}, u32[]{:S(2)}) copy-start(f32[8]{0:T(128)} %refs_11_.3) | copy-start | bytes 100
  14.0 10.7 %collective-permute-start.5 = (bf16[6,3,6,1024]{3,1,0,2:T(4,128)(2,1)S(1)}, bf16[6,3,6,1024]{3,1,0,2:T(4,128)(2,1)S(1)}, u32[]{:S(2)}, u32[]{:S(2)}) collective-permute-start(bf16[6,3,6,1024]{3,1,0,2:T(4,128)(2,1)S(1)} %get-tuple-element.146), channel_id=1, source_target_pairs={{0,112},{16,0},{32,16},{48,32},{64,48},{80,64},{96,80},{112,96},{1... | collective-permute-start | bytes 663560 | tf_op jit(solution)/shard_map/ppermute | solution.py:538
  21.9 11.2 %collective-permute-start.3 = (bf16[162,512]{1,0:T(8,128)(2,1)S(1)}, bf16[162,512]{1,0:T(8,128)(2,1)S(1)}, u32[]{:S(2)}, u32[]{:S(2)}) collective-permute-start(bf16[162,512]{1,0:T(8,128)(2,1)S(1)} %get-tuple-element.78), channel_id=1, source_target_pairs={{0,112},{16,0},{32,16},{48,32},{64,48},{80,64},{96,80},{112,96},{1... | collective-permute-start | bytes 497672 | tf_op jit(solution)/shard_map/ppermute | solution.py:538
  22.0 11.1 %collective-permute-start.4 = (bf16[54,512]{1,0:T(8,128)(2,1)S(1)}, bf16[54,512]{1,0:T(8,128)(2,1)S(1)}, u32[]{:S(2)}, u32[]{:S(2)}) collective-permute-start(bf16[54,512]{1,0:T(8,128)(2,1)S(1)} %get-tuple-element.79), channel_id=1, source_target_pairs={{0,127},{1,112},{2,113},{3,114},{4,115},{5,116},{6,117},{7,118},{8... | collective-permute-start | bytes 165896 | tf_op jit(solution)/shard_map/ppermute | solution.py:548
  25.0 18.1 %slice-start = ((s8[8388608]{0:T(1024)(128)(4,1)}), s8[4194304]{0:T(1024)(128)(4,1)S(1)}, s32[]{:S(2)}) async-start(s8[8388608]{0:T(1024)(128)(4,1)} %bitcast.21), calls=%async_computation.1 | async-start | bytes 8388608
  25.3 7.1 %collective-permute-start.6 = (bf16[3,3,12,1024]{3,1,0,2:T(4,128)(2,1)S(1)}, bf16[3,3,12,1024]{3,1,0,2:T(4,128)(2,1)S(1)}, u32[]{:S(2)}, u32[]{:S(2)}) collective-permute-start(bf16[3,3,12,1024]{3,1,0,2:T(4,128)(2,1)S(1)} %get-tuple-element.144), channel_id=1, source_target_pairs={{0,15},{1,0},{2,1},{3,2},{4,3},{5,4},{6,5},{7,6},{8,7},{9,8},{10,9... | collective-permute-start | bytes 663560 | tf_op jit(solution)/shard_map/ppermute | solution.py:538
  28.0 15.1 %slice-start.1 = ((s8[8388608]{0:T(1024)(128)(4,1)}), s8[4194304]{0:T(1024)(128)(4,1)S(1)}, s32[]{:S(2)}) async-start(s8[8388608]{0:T(1024)(128)(4,1)} %bitcast.21), calls=%async_computation.2 | async-start | bytes 8388608
  32.3 1.2 copy-start.4
  33.1 10.1 %collective-permute-start.7 = (bf16[224,512]{1,0:T(8,128)(2,1)S(1)}, bf16[224,512]{1,0:T(8,128)(2,1)S(1)}, u32[]{:S(2)}, u32[]{:S(2)}) collective-permute-start(bf16[224,512]{1,0:T(8,128)(2,1)S(1)} %get-tuple-element.82), channel_id=1, source_target_pairs={{0,15},{1,0},{2,1},{3,2},{4,3},{5,4},{6,5},{7,6},{8,7},{9,8},{10,9... | collective-permute-start | bytes 688136 | tf_op jit(solution)/shard_map/ppermute | solution.py:538
  33.5 9.7 %copy-start = (bf16[2048,1024]{1,0:T(8,128)(2,1)S(1)}, bf16[2048,1024]{1,0:T(8,128)(2,1)}, u32[]{:S(2)}) copy-start(bf16[2048,1024]{1,0:T(8,128)(2,1)} %mw_ref.1) | copy-start | bytes 12582916
  33.5 9.7 %copy-start.5 = (f32[2048]{0:T(1024)S(1)}, f32[2048]{0:T(1024)}, u32[]{:S(2)}) copy-start(f32[2048]{0:T(1024)} %param.15) | copy-start | bytes 24580
  33.5 9.7 %copy-start.6 = (f32[1024]{0:T(1024)S(1)}, f32[1024]{0:T(1024)}, u32[]{:S(2)}) copy-start(f32[1024]{0:T(1024)} %param.18) | copy-start | bytes 12292
  33.5 9.7 %copy-start.8 = (f32[16]{0:T(128)S(1)}, f32[16]{0:T(128)}, u32[]{:S(2)}) copy-start(f32[16]{0:T(128)} %scale_ref.1) | copy-start | bytes 196
  33.6 23.8 %collective-permute-start.8 = (bf16[216,512]{1,0:T(8,128)(2,1)S(1)}, bf16[216,512]{1,0:T(8,128)(2,1)S(1)}, u32[]{:S(2)}, u32[]{:S(2)}) collective-permute-start(bf16[216,512]{1,0:T(8,128)(2,1)S(1)} %get-tuple-element.93), channel_id=1, source_target_pairs={{0,15},{1,0},{2,1},{3,2},{4,3},{5,4},{6,5},{7,6},{8,7},{9,8},{10,9... | collective-permute-start | bytes 663560 | tf_op jit(solution)/shard_map/ppermute | solution.py:538
  37.3 20.1 %collective-permute-start.9 = (bf16[162,512]{1,0:T(8,128)(2,1)S(1)}, bf16[162,512]{1,0:T(8,128)(2,1)S(1)}, u32[]{:S(2)}, u32[]{:S(2)}) collective-permute-start(bf16[162,512]{1,0:T(8,128)(2,1)S(1)} %get-tuple-element.94), channel_id=1, source_target_pairs={{0,112},{16,0},{32,16},{48,32},{64,48},{80,64},{96,80},{112,96},{1... | collective-permute-start | bytes 497672 | tf_op jit(solution)/shard_map/ppermute | solution.py:538
  43.0 14.5 %collective-permute-start.10 = (bf16[54,512]{1,0:T(8,128)(2,1)S(1)}, bf16[54,512]{1,0:T(8,128)(2,1)S(1)}, u32[]{:S(2)}, u32[]{:S(2)}) collective-permute-start(bf16[54,512]{1,0:T(8,128)(2,1)S(1)} %get-tuple-element.95), channel_id=1, source_target_pairs={{0,127},{1,112},{2,113},{3,114},{4,115},{5,116},{6,117},{7,118},{8... | collective-permute-start | bytes 165896 | tf_op jit(solution)/shard_map/ppermute | solution.py:548
  57.5 6.0 %collective-permute-start.11 = (bf16[216,512]{1,0:T(8,128)(2,1)S(1)}, bf16[216,512]{1,0:T(8,128)(2,1)S(1)}, u32[]{:S(2)}, u32[]{:S(2)}) collective-permute-start(bf16[216,512]{1,0:T(8,128)(2,1)S(1)} %get-tuple-element.96), channel_id=1, source_target_pairs={{0,1},{1,2},{2,3},{3,4},{4,5},{5,6},{6,7},{7,8},{8,9},{9,10},{10,1... | collective-permute-start | bytes 663560 | tf_op jit(solution)/shard_map/ppermute | solution.py:538
  58.7 17.3 %collective-permute-start.14 = (bf16[162,512]{1,0:T(8,128)(2,1)S(1)}, bf16[162,512]{1,0:T(8,128)(2,1)S(1)}, u32[]{:S(2)}, u32[]{:S(2)}) collective-permute-start(bf16[162,512]{1,0:T(8,128)(2,1)S(1)} %get-tuple-element.113), channel_id=1, source_target_pairs={{0,16},{16,32},{32,48},{48,64},{64,80},{80,96},{96,112},{112,0},{1... | collective-permute-start | bytes 497672 | tf_op jit(solution)/shard_map/ppermute | solution.py:538
  61.7 14.3 %collective-permute-start.15 = (bf16[54,512]{1,0:T(8,128)(2,1)S(1)}, bf16[54,512]{1,0:T(8,128)(2,1)S(1)}, u32[]{:S(2)}, u32[]{:S(2)}) collective-permute-start(bf16[54,512]{1,0:T(8,128)(2,1)S(1)} %get-tuple-element.114), channel_id=1, source_target_pairs={{0,17},{1,18},{2,19},{3,20},{4,21},{5,22},{6,23},{7,24},{8,25},{9,... | collective-permute-start | bytes 165896 | tf_op jit(solution)/shard_map/ppermute | solution.py:548
  63.7 11.1 %collective-permute-start.12 = (bf16[6,3,6,1024]{3,1,0,2:T(4,128)(2,1)S(1)}, bf16[6,3,6,1024]{3,1,0,2:T(4,128)(2,1)S(1)}, u32[]{:S(2)}, u32[]{:S(2)}) collective-permute-start(bf16[6,3,6,1024]{3,1,0,2:T(4,128)(2,1)S(1)} %copy.17), channel_id=1, source_target_pairs={{0,16},{16,32},{32,48},{48,64},{64,80},{80,96},{96,112},{112,0},{1... | collective-permute-start | bytes 663560 | tf_op jit(solution)/shard_map/ppermute | solution.py:538
  82.6 5.6 %collective-permute-start.16 = (bf16[512,1024]{1,0:T(8,128)(2,1)S(1)}, bf16[512,1024]{1,0:T(8,128)(2,1)S(1)}, u32[]{:S(2)}, u32[]{:S(2)}) collective-permute-start(bf16[512,1024]{1,0:T(8,128)(2,1)S(1)} %get-tuple-element.123), channel_id=1, source_target_pairs={{0,1},{1,0},{2,3},{3,2},{4,5},{5,4},{6,7},{7,6},{8,9},{9,8},{10,11... | collective-permute-start | bytes 3145736 | tf_op jit(solution)/shard_map/ppermute | solution.py:615
  88.3 6.2 %copy-start.10 = (bf16[6,3,12,1024]{3,1,0,2:T(4,128)(2,1)S(1)}, bf16[6,3,12,1024]{3,1,0,2:T(4,128)(2,1)}, u32[]{:S(2)}) copy-start(bf16[6,3,12,1024]{3,1,0,2:T(4,128)(2,1)} %pad_maximum_fusion.2) | copy-start | bytes 1327108
  89.7 24.9 %all-to-all-start = ((bf16[64,8,1024]{2,1,0:T(8,128)(2,1)}), bf16[64,8,1024]{2,1,0:T(8,128)(2,1)S(1)}, u32[]{:S(2)}, u32[]{:S(2)}) async-start(bf16[64,8,1024]{2,1,0:T(8,128)(2,1)} %fusion), calls=%async_computation | async-start | bytes 2097152 | tf_op jit(solution)/shard_map/all_to_all | solution.py:563
  95.5 19.2 %collective-permute-start.13 = (bf16[3,3,12,1024]{3,1,0,2:T(4,128)(2,1)}, bf16[3,3,12,1024]{3,1,0,2:T(4,128)(2,1)S(1)}, u32[]{:S(2)}, u32[]{:S(2)}) collective-permute-start(bf16[3,3,12,1024]{3,1,0,2:T(4,128)(2,1)} %get-tuple-element.139), channel_id=1, source_target_pairs={{0,1},{1,2},{2,3},{3,4},{4,5},{5,6},{6,7},{7,8},{8,9},{9,10},{10,1... | collective-permute-start | bytes 663560 | tf_op jit(solution)/shard_map/ppermute | solution.py:538
  97.0 17.8 %collective-permute-start.17 = (bf16[216,512]{1,0:T(8,128)(2,1)S(1)}, bf16[216,512]{1,0:T(8,128)(2,1)S(1)}, u32[]{:S(2)}, u32[]{:S(2)}) collective-permute-start(bf16[216,512]{1,0:T(8,128)(2,1)S(1)} %get-tuple-element.133), channel_id=1, source_target_pairs={{0,1},{1,2},{2,3},{3,4},{4,5},{5,6},{6,7},{7,8},{8,9},{9,10},{10,1... | collective-permute-start | bytes 663560 | tf_op jit(solution)/shard_map/ppermute | solution.py:538
  97.0 21.4 %collective-permute-start.18 = (bf16[162,512]{1,0:T(8,128)(2,1)S(1)}, bf16[162,512]{1,0:T(8,128)(2,1)S(1)}, u32[]{:S(2)}, u32[]{:S(2)}) collective-permute-start(bf16[162,512]{1,0:T(8,128)(2,1)S(1)} %get-tuple-element.135), channel_id=1, source_target_pairs={{0,16},{16,32},{32,48},{48,64},{64,80},{80,96},{96,112},{112,0},{1... | collective-permute-start | bytes 497672 | tf_op jit(solution)/shard_map/ppermute | solution.py:538
  99.7 20.3 %collective-permute-start.19 = (bf16[54,512]{1,0:T(8,128)(2,1)S(1)}, bf16[54,512]{1,0:T(8,128)(2,1)S(1)}, u32[]{:S(2)}, u32[]{:S(2)}) collective-permute-start(bf16[54,512]{1,0:T(8,128)(2,1)S(1)} %get-tuple-element.137), channel_id=1, source_target_pairs={{0,17},{1,18},{2,19},{3,20},{4,21},{5,22},{6,23},{7,24},{8,25},{9,... | collective-permute-start | bytes 165896 | tf_op jit(solution)/shard_map/ppermute | solution.py:548
  120.1 4.8 %collective-permute-start.20 = (f32[4,1024]{1,0:T(4,128)S(1)}, f32[4,1024]{1,0:T(4,128)S(1)}, u32[]{:S(2)}, u32[]{:S(2)}) collective-permute-start(f32[4,1024]{1,0:T(4,128)S(1)} %slice_select_fusion), channel_id=1, source_target_pairs={{0,1},{1,0},{2,3},{3,2},{4,5},{5,4},{6,7},{7,6},{8,9},{9,8},{10,11... | collective-permute-start | bytes 49160 | tf_op jit(solution)/shard_map/ppermute | solution.py:570
  122.3 1.3 %copy-start.11 = (bf16[3,3,12,1024]{3,1,0,2:T(4,128)(2,1)S(1)}, bf16[3,3,12,1024]{3,1,0,2:T(4,128)(2,1)}, u32[]{:S(2)}) copy-start(bf16[3,3,12,1024]{3,1,0,2:T(4,128)(2,1)} %get-tuple-element.140) | copy-start | bytes 663556

commit v3 on v2

--- a/solution.py
+++ b/solution.py
@@ -567,8 +567,9 @@
 def own_rows(total, core):
     first = core == 0
     mine = jnp.where(first, total[:4], total[4:])
-    other = lax.ppermute(jnp.where(first, total[4:], total[:4]), "core", [(0, 1), (1, 0)])
-    return jnp.concatenate([jnp.where(first, mine, other), jnp.where(first, other, mine)], 1)
+    leaving = jnp.where(first, total[4:], total[:4])
+    other = lax.ppermute(leaving, "core", [(0, 1), (1, 0)])
+    return jnp.concatenate([jnp.where(first, mine, other), jnp.where(first, other, mine)], 1), leaving
 
 
 def on_device(
@@ -620,10 +621,10 @@
     sent, keep, g0 = lax.optimization_barrier((sent, keep, g0))
     part = (keep.astype(F32) + sent.astype(F32)).astype(BF16)
     total = chip_sum(part)
-    share = own_rows(total, core[0])
-    lat, lon, corner = (after(block, total) for block in (lat, lon, corner))
+    share, leaving = own_rows(total, core[0])
+    lat, lon, corner = (after(block, leaving) for block in (lat, lon, corner))
     grad_input = assemble((g0, g1, lat, lon, corner)).reshape(LAT, LEV, LON, D1)
-    coarse_out = jnp.concatenate([after(other, total), own], 0)
+    coarse_out = jnp.concatenate([after(other, leaving), own], 0)
     return coarse_out.transpose(2, 0, 1, 3), grad_input.transpose(2, 0, 1, 3), share
 
 

time: 126 us -> 124 us (0.984)
  waiting for transfers between devices: 22.7 us -> 20 us
    ppermute x14, waiting for transfers between devices: 8.9 us -> 6.29 us  [moved(): return lax.ppermute(block, axis, ring(lax.axis_size(axis), step))]
  transfers between devices with their start and end apart: 22 -> 22, of which waited for: 4 -> 4; matrix products, arithmetic and copies ran while one was open for 4% -> 5% of each run, Pallas kernels for 27% -> 27%
where the time goes in v3:
time: 124 us; the launch traced here: 123 us
  starting transfers between devices  52.4 us (42%)
  Pallas kernels  40.1 us (32%)
  waiting for transfers between devices  20 us (16%)
  other arithmetic  5.38 us (4%)
  local copies, waits for them, and re-layouts  4.33 us (3%)
    pallas_call x12, Pallas kernels, call(): pl.pallas_call(kernel, out_shape=[jax.ShapeDtypeStruct(shape, kind) for s...  40.1 us
    ppermute x14, starting transfers between devices, moved(): return lax.ppermute(block, axis, ring(lax.axis_size(axis), step))  33.4 us
    all_to_all x1, waiting for transfers between devices, chip_sum(): pieces = lax.all_to_all(part.reshape(64, 8, 2 * D1), ('lon', 'chip'), 0, 0)  12.1 us
    ppermute x5, starting transfers between devices, moved_both(): return lax.ppermute(block, ('lon', *LAT_AXES), route)  8.79 us
    ppermute x14, waiting for transfers between devices, moved(): return lax.ppermute(block, axis, ring(lax.axis_size(axis), step))  6.29 us
    all_to_all x1, starting transfers between devices, chip_sum(): pieces = lax.all_to_all(part.reshape(64, 8, 2 * D1), ('lon', 'chip'), 0, 0)  4.8 us
    ppermute x1, starting transfers between devices, on_device(): sent = lax.ppermute(send, 'core', [(0, 1), (1, 0)])  2.83 us
    ppermute x1, starting transfers between devices, own_rows(): other = lax.ppermute(leaving, 'core', [(0, 1), (1, 0)])  2.61 us
  transfers between devices with their start and end apart: 22, of which 4 were waited for; matrix products, arithmetic and copies ran while one was open for 5% of the time, Pallas kernels for 27%

profile of v3, /device:TPU:1, one launch (start us, length us, event | category | flops | bytes accessed | tf_op | source)
XLA Modules:
  0.0 123.2 jit_solution(3185369966535002527)
XLA Ops:
  0.6 0.0 copy-start.2
  0.6 1.2 copy-done.2
  1.8 0.1 edges.2
  1.9 1.5 %collective-permute-start = (bf16[216,512]{1,0:T(8,128)(2,1)S(1)}, bf16[216,512]{1,0:T(8,128)(2,1)S(1)}, u32[]{:S(2)}, u32[]{:S(2)}) collective-permute-start(bf16[216,512]{1,0:T(8,128)(2,1)S(1)} %get-tuple-element.71), channel_id=1, source_target_pairs={{0,15},{1,0},{2,1},{3,2},{4,3},{5,4},{6,5},{7,6},{8,7},{9,8},{10,9... | collective-permute-start | bytes 663560 | tf_op jit(solution)/shard_map/ppermute | solution.py:538
  3.4 6.1 %collective-permute-start.1 = (bf16[162,512]{1,0:T(8,128)(2,1)S(1)}, bf16[162,512]{1,0:T(8,128)(2,1)S(1)}, u32[]{:S(2)}, u32[]{:S(2)}) collective-permute-start(bf16[162,512]{1,0:T(8,128)(2,1)S(1)} %get-tuple-element.73), channel_id=1, source_target_pairs={{0,112},{16,0},{32,16},{48,32},{64,48},{80,64},{96,80},{112,96},{1... | collective-permute-start | bytes 497672 | tf_op jit(solution)/shard_map/ppermute | solution.py:538
  9.5 3.2 %collective-permute-start.2 = (bf16[54,512]{1,0:T(8,128)(2,1)S(1)}, bf16[54,512]{1,0:T(8,128)(2,1)S(1)}, u32[]{:S(2)}, u32[]{:S(2)}) collective-permute-start(bf16[54,512]{1,0:T(8,128)(2,1)S(1)} %get-tuple-element.74), channel_id=1, source_target_pairs={{0,127},{1,112},{2,113},{3,114},{4,115},{5,116},{6,117},{7,118},{8... | collective-permute-start | bytes 165896 | tf_op jit(solution)/shard_map/ppermute | solution.py:548
  12.7 0.0 copy-start.9
  12.7 0.5 turn.1.refs_2_.refs_5_
  13.2 0.0 collective-permute-done.refs_1_
  13.2 0.6 copy-done.12
  13.8 0.2 fusion.4
  14.0 3.5 %collective-permute-start.5 = (bf16[6,3,6,1024]{3,1,0,2:T(4,128)(2,1)S(1)}, bf16[6,3,6,1024]{3,1,0,2:T(4,128)(2,1)S(1)}, u32[]{:S(2)}, u32[]{:S(2)}) collective-permute-start(bf16[6,3,6,1024]{3,1,0,2:T(4,128)(2,1)S(1)} %get-tuple-element.146), channel_id=1, source_target_pairs={{0,112},{16,0},{32,16},{48,32},{64,48},{80,64},{96,80},{112,96},{1... | collective-permute-start | bytes 663560 | tf_op jit(solution)/shard_map/ppermute | solution.py:538
  17.4 4.4 %fine_forward_0.1 = (bf16[2,216,512]{2,1,0:T(8,128)(2,1)S(1)}, bf16[112,512]{1,0:T(8,128)(2,1)S(1)}, bf16[162,512]{1,0:T(8,128)(2,1)S(1)}, bf16[54,512]{1,0:T(8,...) custom-call(bf16[864,512]{1,0:T(8,128)(2,1)S(1)} %bitcast.26, ...), custom_call_target="tpu_custom_call" | custom-call | flops 10000000000 | bytes 4194304 | tf_op jit(solution)/shard_map/fine_forward_0/pallas_call | solution.py:429
  21.9 0.1 collective-permute-start.3
  22.0 2.7 %collective-permute-start.4 = (bf16[54,512]{1,0:T(8,128)(2,1)S(1)}, bf16[54,512]{1,0:T(8,128)(2,1)S(1)}, u32[]{:S(2)}, u32[]{:S(2)}) collective-permute-start(bf16[54,512]{1,0:T(8,128)(2,1)S(1)} %get-tuple-element.79), channel_id=1, source_target_pairs={{0,127},{1,112},{2,113},{3,114},{4,115},{5,116},{6,117},{7,118},{8... | collective-permute-start | bytes 165896 | tf_op jit(solution)/shard_map/ppermute | solution.py:548
  24.7 0.0 collective-permute-done.5
  24.7 0.4 pad_maximum_fusion
  25.0 0.0 slice-start
  25.1 0.2 fusion.3
  25.3 2.8 %collective-permute-start.6 = (bf16[3,3,12,1024]{3,1,0,2:T(4,128)(2,1)S(1)}, bf16[3,3,12,1024]{3,1,0,2:T(4,128)(2,1)S(1)}, u32[]{:S(2)}, u32[]{:S(2)}) collective-permute-start(bf16[3,3,12,1024]{3,1,0,2:T(4,128)(2,1)S(1)} %get-tuple-element.144), channel_id=1, source_target_pairs={{0,15},{1,0},{2,1},{3,2},{4,3},{5,4},{6,5},{7,6},{8,7},{9,8},{10,9... | collective-permute-start | bytes 663560 | tf_op jit(solution)/shard_map/ppermute | solution.py:538
  28.0 4.3 %fine_forward_1.1 = (bf16[2,216,512]{2,1,0:T(8,128)(2,1)S(1)}, bf16[224,512]{1,0:T(8,128)(2,1)S(1)}, bf16[2,216,512]{2,1,0:T(8,128)(2,1)S(1)}, bf16[2,1536,216]{...) custom-call(bf16[864,512]{1,0:T(8,128)(2,1)S(1)} %bitcast.27, ...), custom_call_target="tpu_custom_call" | custom-call | flops 10000000000 | bytes 4194304 | tf_op jit(solution)/shard_map/fine_forward_1/pallas_call | solution.py:429
  32.3 0.0 copy-start.4
  32.3 0.4 pad_maximum_fusion.1
  32.7 0.3 copy.14
  33.1 0.0 collective-permute-done.3.lon_ref
  33.1 0.1 collective-permute-start.7
  33.2 0.3 copy-done.4
  33.5 0.1 edges.3
  33.6 3.7 %collective-permute-start.8 = (bf16[216,512]{1,0:T(8,128)(2,1)S(1)}, bf16[216,512]{1,0:T(8,128)(2,1)S(1)}, u32[]{:S(2)}, u32[]{:S(2)}) collective-permute-start(bf16[216,512]{1,0:T(8,128)(2,1)S(1)} %get-tuple-element.93), channel_id=1, source_target_pairs={{0,15},{1,0},{2,1},{3,2},{4,3},{5,4},{6,5},{7,6},{8,7},{9,8},{10,9... | collective-permute-start | bytes 663560 | tf_op jit(solution)/shard_map/ppermute | solution.py:538
  37.3 5.7 %collective-permute-start.9 = (bf16[162,512]{1,0:T(8,128)(2,1)S(1)}, bf16[162,512]{1,0:T(8,128)(2,1)S(1)}, u32[]{:S(2)}, u32[]{:S(2)}) collective-permute-start(bf16[162,512]{1,0:T(8,128)(2,1)S(1)} %get-tuple-element.94), channel_id=1, source_target_pairs={{0,112},{16,0},{32,16},{48,32},{64,48},{80,64},{96,80},{112,96},{1... | collective-permute-start | bytes 497672 | tf_op jit(solution)/shard_map/ppermute | solution.py:538
  43.0 0.2 collective-permute-start.10
  43.2 0.0 collective-permute-done.7.lat_ref
  43.2 14.2 %coarse_both.1 = (bf16[1024,216]{1,0:T(8,128)(2,1)S(1)}, bf16[216,1024]{1,0:T(8,128)(2,1)S(1)}, bf16[864,512]{1,0:T(8,128)(2,1)S(1)}, bf16[216,512]{1,0:T(8,128)...) custom-call(bf16[2,216,512]{2,1,0:T(8,128)(2,1)S(1)} %get-tuple-element.72.y0_ref, ...), custom_call_target="tpu_custom_call" | custom-call | flops 20000000000 | bytes 4194304 | tf_op jit(solution)/shard_map/coarse_both/pallas_call | solution.py:429
  57.4 0.0 collective-permute-done.9.refs_4_
  57.5 1.3 %collective-permute-start.11 = (bf16[216,512]{1,0:T(8,128)(2,1)S(1)}, bf16[216,512]{1,0:T(8,128)(2,1)S(1)}, u32[]{:S(2)}, u32[]{:S(2)}) collective-permute-start(bf16[216,512]{1,0:T(8,128)(2,1)S(1)} %get-tuple-element.96), channel_id=1, source_target_pairs={{0,1},{1,2},{2,3},{3,4},{4,5},{5,6},{6,7},{7,8},{8,9},{9,10},{10,1... | collective-permute-start | bytes 663560 | tf_op jit(solution)/shard_map/ppermute | solution.py:538
  58.7 3.0 %collective-permute-start.14 = (bf16[162,512]{1,0:T(8,128)(2,1)S(1)}, bf16[162,512]{1,0:T(8,128)(2,1)S(1)}, u32[]{:S(2)}, u32[]{:S(2)}) collective-permute-start(bf16[162,512]{1,0:T(8,128)(2,1)S(1)} %get-tuple-element.113), channel_id=1, source_target_pairs={{0,16},{16,32},{32,48},{48,64},{64,80},{80,96},{96,112},{112,0},{1... | collective-permute-start | bytes 497672 | tf_op jit(solution)/shard_map/ppermute | solution.py:538
  61.7 0.7 coarse_out.1
  62.5 0.9 normed.1
  63.4 0.1 fusion.2
  63.5 0.2 copy.17
  63.7 1.5 %collective-permute-start.12 = (bf16[6,3,6,1024]{3,1,0,2:T(4,128)(2,1)S(1)}, bf16[6,3,6,1024]{3,1,0,2:T(4,128)(2,1)S(1)}, u32[]{:S(2)}, u32[]{:S(2)}) collective-permute-start(bf16[6,3,6,1024]{3,1,0,2:T(4,128)(2,1)S(1)} %copy.17), channel_id=1, source_target_pairs={{0,16},{16,32},{32,48},{48,64},{64,80},{80,96},{96,112},{112,0},{1... | collective-permute-start | bytes 663560 | tf_op jit(solution)/shard_map/ppermute | solution.py:538
  65.2 4.2 %fine_backward_1.1 = (bf16[2,1536,256]{2,1,0:T(8,128)(2,1)S(1)}, bf16[2,216,512]{2,1,0:T(8,128)(2,1)S(1)}) custom-call(bf16[864,512]{1,0:T(8,128)(2,1)S(1)} %get-tuple-element.86.refs_0_, bf16[216,512]{1,0:T(8,128)(2,1)S(1)} %collective-permute-done.11.refs_1_, bf16[864,512]{1,0:T(8,128)(2,1)S(1)} %bitcast.29, ...), custom_call_target="tpu_custom_call" | custom-call | flops 10000000000 | bytes 4194304 | tf_op jit(solution)/shard_map/fine_backward_1/pallas_call | solution.py:429
  69.4 0.2 copy.18
  69.6 5.2 %collective-permute-done.12 = bf16[6,3,6,1024]{3,1,0,2:T(4,128)(2,1)S(1)} collective-permute-done((bf16[6,3,6,1024]{3,1,0,2:T(4,128)(2,1)S(1)}, bf16[6,3,6,1024]{3,1,0,2:T(4,128)(2,1)S(1)}, u32[]{:S(2)}, u32[]{:S(2)}) %collective-permute-start.12) | collective-permute-done | bytes 221216 | tf_op jit(solution)/shard_map/ppermute | solution.py:538
  74.8 1.2 pad_maximum_fusion.2
  76.0 6.6 %fine_backward_0.1 = (bf16[2,1536,256]{2,1,0:T(8,128)(2,1)S(1)}, bf16[2,216,512]{2,1,0:T(8,128)(2,1)S(1)}, bf16[512,1024]{1,0:T(8,128)(2,1)S(1)}, bf16[512,1024]{1,0:T(8,128)(2,1)S(1)}) custom-call(bf16[864,512]{1,0:T(8,128)(2,1)S(1)} %get-tuple-element.86.refs_0_, bf16[216,512]{1,0:T(8,128)(2,1)S(1)} %collective-permute-done.11.refs_1_, ...), custom_call_target="tpu_custom_call" | custom-call | flops 10000000000 | bytes 4194304 | tf_op jit(solution)/shard_map/fine_backward_0/pallas_call | solution.py:429
  82.6 2.8 %collective-permute-start.16 = (bf16[512,1024]{1,0:T(8,128)(2,1)S(1)}, bf16[512,1024]{1,0:T(8,128)(2,1)S(1)}, u32[]{:S(2)}, u32[]{:S(2)}) collective-permute-start(bf16[512,1024]{1,0:T(8,128)(2,1)S(1)} %get-tuple-element.123), channel_id=1, source_target_pairs={{0,1},{1,0},{2,3},{3,2},{4,5},{5,4},{6,7},{7,6},{8,9},{9,8},{10,11... | collective-permute-start | bytes 3145736 | tf_op jit(solution)/shard_map/ppermute | solution.py:616
  85.5 2.8 %fine_input.1 = (bf16[2,216,512]{2,1,0:T(8,128)(2,1)S(1)}, bf16[2,216,512]{2,1,0:T(8,128)(2,1)S(1)}, bf16[216,512]{1,0:T(8,128)(2,1)S(1)}, bf16[162,512]{1,0:T(8,128)(2,1)S(1)}, bf16[54,512]{1,0:T(8,128)(2,1)S(1)}) custom-call(bf16[2,1536,256]{2,1,0:T(8,128)(2,1)S(1)} %get-tuple-element.125.gq0_ref, ...), custom_call_target="tpu_custom_call" | custom-call | flops 6000000000 | bytes 4194304 | tf_op jit(solution)/shard_map/fine_input/pallas_call | solution.py:429
  88.3 0.0 copy-start.10
  88.3 1.4 %fusion = bf16[64,8,1024]{2,1,0:T(8,128)(2,1)} fusion(bf16[512,1024]{1,0:T(8,128)(2,1)S(1)} %collective-permute-done.16, bf16[512,1024]{1,0:T(8,128)(2,1)S(1)} %get-tuple-element.128), kind=kLoop, calls=%fused_computation.2 | loop fusion | flops 2097152 | bytes 3145728 | tf_op jit(solution)/shard_map/reshape | solution.py:563
  89.7 4.8 %all-to-all-start = ((bf16[64,8,1024]{2,1,0:T(8,128)(2,1)}), bf16[64,8,1024]{2,1,0:T(8,128)(2,1)S(1)}, u32[]{:S(2)}, u32[]{:S(2)}) async-start(bf16[64,8,1024]{2,1,0:T(8,128)(2,1)} %fusion), calls=%async_computation | async-start | bytes 2097152 | tf_op jit(solution)/shard_map/all_to_all | solution.py:563
  94.5 1.0 fusion.1
  95.5 1.5 %collective-permute-start.13 = (bf16[3,3,12,1024]{3,1,0,2:T(4,128)(2,1)}, bf16[3,3,12,1024]{3,1,0,2:T(4,128)(2,1)S(1)}, u32[]{:S(2)}, u32[]{:S(2)}) collective-permute-start(bf16[3,3,12,1024]{3,1,0,2:T(4,128)(2,1)} %get-tuple-element.139), channel_id=1, source_target_pairs={{0,1},{1,2},{2,3},{3,4},{4,5},{5,6},{6,7},{7,8},{8,9},{9,10},{10,1... | collective-permute-start | bytes 663560 | tf_op jit(solution)/shard_map/ppermute | solution.py:538
  97.0 0.0 collective-permute-start.17
  97.0 2.7 %collective-permute-start.18 = (bf16[162,512]{1,0:T(8,128)(2,1)S(1)}, bf16[162,512]{1,0:T(8,128)(2,1)S(1)}, u32[]{:S(2)}, u32[]{:S(2)}) collective-permute-start(bf16[162,512]{1,0:T(8,128)(2,1)S(1)} %get-tuple-element.135), channel_id=1, source_target_pairs={{0,16},{16,32},{32,48},{48,64},{64,80},{80,96},{96,112},{112,0},{1... | collective-permute-start | bytes 497672 | tf_op jit(solution)/shard_map/ppermute | solution.py:538
  99.7 2.7 %collective-permute-start.19 = (bf16[54,512]{1,0:T(8,128)(2,1)S(1)}, bf16[54,512]{1,0:T(8,128)(2,1)S(1)}, u32[]{:S(2)}, u32[]{:S(2)}) collective-permute-start(bf16[54,512]{1,0:T(8,128)(2,1)S(1)} %get-tuple-element.137), channel_id=1, source_target_pairs={{0,17},{1,18},{2,19},{3,20},{4,21},{5,22},{6,23},{7,24},{8,25},{9,... | collective-permute-start | bytes 165896 | tf_op jit(solution)/shard_map/ppermute | solution.py:548
  102.5 12.1 %all-to-all-done = bf16[64,8,1024]{2,1,0:T(8,128)(2,1)S(1)} async-done(((bf16[64,8,1024]{2,1,0:T(8,128)(2,1)}), bf16[64,8,1024]{2,1,0:T(8,128)(2,1)S(1)}, u32[]{:S(2)}, u32[]{:S(2)}) %all-to-all-start) | async-done | bytes 1048608 | tf_op jit(solution)/shard_map/all_to_all | solution.py:563
  114.6 0.2 convert_reduce_fusion
  114.8 2.6 %collective-permute-start.20 = (f32[4,1024]{1,0:T(4,128)S(1)}, f32[4,1024]{1,0:T(4,128)S(1)}, u32[]{:S(2)}, u32[]{:S(2)}) collective-permute-start(f32[4,1024]{1,0:T(4,128)S(1)} %slice_select_fusion.1), channel_id=1, source_target_pairs={{0,1},{1,0},{2,3},{3,2},{4,5},{5,4},{6,7},{7,6},{8,9},{9,8},{10,11... | collective-permute-start | bytes 49160 | tf_op jit(solution)/shard_map/ppermute | solution.py:571
  117.4 1.1 collective-permute-done.18.lon_ref
  118.4 1.6 %collective-permute-done.19.corner_ref = bf16[54,512]{1,0:T(8,128)(2,1)S(1)} collective-permute-done((bf16[54,512]{1,0:T(8,128)(2,1)S(1)}, bf16[54,512]{1,0:T(8,128)(2,1)S(1)}, u32[]{:S(2)}, u32[]{:S(2)}) %collective-permute-start.19) | collective-permute-done | bytes 55328 | tf_op jit(solution)/shard_map/ppermute | solution.py:548
  120.1 1.3 %assemble.1 = bf16[864,512]{1,0:T(8,128)(2,1)} custom-call(bf16[2,216,512]{2,1,0:T(8,128)(2,1)S(1)} %get-tuple-element.131.g0_ref, bf16[2,216,512]{2,1,0:T(8,128)(2,1)S(1)} %get-tuple-element.132.g1_ref, bf16[216,512]{1,0:T(8,128)(2,1)S(1)} %collective-permute-done.17.lat_ref, bf16[162,512]{1,0:T(8,128)(2,1)S(1)} %collective-permute-done.18.lon_ref, ...), custom_call_target="tpu_custom_call" | custom-call | flops 2000000000 | bytes 4194304 | tf_op jit(solution)/shard_map/assemble/pallas_call | solution.py:429
  121.4 1.2 maximum_bitcast_fusion
  122.6 0.6 pad_maximum_fusion.3
  (39 shorter events, 0.1 us)
Async XLA Ops:
  0.6 1.2 copy-start.2
  1.8 10.9 %copy-start.1 = (bf16[512,2048]{1,0:T(8,128)(2,1)S(1)}, bf16[512,2048]{1,0:T(8,128)(2,1)}, u32[]{:S(2)}) copy-start(bf16[512,2048]{1,0:T(8,128)(2,1)} %w_ref.3) | copy-start | bytes 6291460
  1.9 11.3 %collective-permute-start = (bf16[216,512]{1,0:T(8,128)(2,1)S(1)}, bf16[216,512]{1,0:T(8,128)(2,1)S(1)}, u32[]{:S(2)}, u32[]{:S(2)}) collective-permute-start(bf16[216,512]{1,0:T(8,128)(2,1)S(1)} %get-tuple-element.71), channel_id=1, source_target_pairs={{0,15},{1,0},{2,1},{3,2},{4,3},{5,4},{6,5},{7,6},{8,7},{9,8},{10,9... | collective-permute-start | bytes 663560 | tf_op jit(solution)/shard_map/ppermute | solution.py:538
  3.4 24.7 %collective-permute-start.1 = (bf16[162,512]{1,0:T(8,128)(2,1)S(1)}, bf16[162,512]{1,0:T(8,128)(2,1)S(1)}, u32[]{:S(2)}, u32[]{:S(2)}) collective-permute-start(bf16[162,512]{1,0:T(8,128)(2,1)S(1)} %get-tuple-element.73), channel_id=1, source_target_pairs={{0,112},{16,0},{32,16},{48,32},{64,48},{80,64},{96,80},{112,96},{1... | collective-permute-start | bytes 497672 | tf_op jit(solution)/shard_map/ppermute | solution.py:538
  9.5 18.5 %collective-permute-start.2 = (bf16[54,512]{1,0:T(8,128)(2,1)S(1)}, bf16[54,512]{1,0:T(8,128)(2,1)S(1)}, u32[]{:S(2)}, u32[]{:S(2)}) collective-permute-start(bf16[54,512]{1,0:T(8,128)(2,1)S(1)} %get-tuple-element.74), channel_id=1, source_target_pairs={{0,127},{1,112},{2,113},{3,114},{4,115},{5,116},{6,117},{7,118},{8... | collective-permute-start | bytes 165896 | tf_op jit(solution)/shard_map/ppermute | solution.py:548
  12.7 1.1 copy-start.12
  12.7 4.7 %copy-start.3 = (bf16[24,12,3,512]{3,0,2,1:T(8,128)(2,1)S(1)}, bf16[24,12,3,512]{3,0,2,1:T(8,128)(2,1)}, u32[]{:S(2)}) copy-start(bf16[24,12,3,512]{3,0,2,1:T(8,128)(2,1)} %param.11) | copy-start | bytes 2654212
  12.7 4.7 %copy-start.7 = (f32[512]{0:T(512)S(1)}, f32[512]{0:T(512)}, u32[]{:S(2)}) copy-start(f32[512]{0:T(512)} %param.13) | copy-start | bytes 6148
  12.7 4.7 %copy-start.9 = (f32[8]{0:T(128)S(1)}, f32[8]{0:T(128)}, u32[]{:S(2)}) copy-start(f32[8]{0:T(128)} %refs_11_.3) | copy-start | bytes 100
  14.0 10.7 %collective-permute-start.5 = (bf16[6,3,6,1024]{3,1,0,2:T(4,128)(2,1)S(1)}, bf16[6,3,6,1024]{3,1,0,2:T(4,128)(2,1)S(1)}, u32[]{:S(2)}, u32[]{:S(2)}) collective-permute-start(bf16[6,3,6,1024]{3,1,0,2:T(4,128)(2,1)S(1)} %get-tuple-element.146), channel_id=1, source_target_pairs={{0,112},{16,0},{32,16},{48,32},{64,48},{80,64},{96,80},{112,96},{1... | collective-permute-start | bytes 663560 | tf_op jit(solution)/shard_map/ppermute | solution.py:538
  21.9 11.2 %collective-permute-start.3 = (bf16[162,512]{1,0:T(8,128)(2,1)S(1)}, bf16[162,512]{1,0:T(8,128)(2,1)S(1)}, u32[]{:S(2)}, u32[]{:S(2)}) collective-permute-start(bf16[162,512]{1,0:T(8,128)(2,1)S(1)} %get-tuple-element.78), channel_id=1, source_target_pairs={{0,112},{16,0},{32,16},{48,32},{64,48},{80,64},{96,80},{112,96},{1... | collective-permute-start | bytes 497672 | tf_op jit(solution)/shard_map/ppermute | solution.py:538
  22.0 11.1 %collective-permute-start.4 = (bf16[54,512]{1,0:T(8,128)(2,1)S(1)}, bf16[54,512]{1,0:T(8,128)(2,1)S(1)}, u32[]{:S(2)}, u32[]{:S(2)}) collective-permute-start(bf16[54,512]{1,0:T(8,128)(2,1)S(1)} %get-tuple-element.79), channel_id=1, source_target_pairs={{0,127},{1,112},{2,113},{3,114},{4,115},{5,116},{6,117},{7,118},{8... | collective-permute-start | bytes 165896 | tf_op jit(solution)/shard_map/ppermute | solution.py:548
  25.0 18.1 %slice-start = ((s8[8388608]{0:T(1024)(128)(4,1)}), s8[4194304]{0:T(1024)(128)(4,1)S(1)}, s32[]{:S(2)}) async-start(s8[8388608]{0:T(1024)(128)(4,1)} %bitcast.21), calls=%async_computation.1 | async-start | bytes 8388608
  25.3 7.1 %collective-permute-start.6 = (bf16[3,3,12,1024]{3,1,0,2:T(4,128)(2,1)S(1)}, bf16[3,3,12,1024]{3,1,0,2:T(4,128)(2,1)S(1)}, u32[]{:S(2)}, u32[]{:S(2)}) collective-permute-start(bf16[3,3,12,1024]{3,1,0,2:T(4,128)(2,1)S(1)} %get-tuple-element.144), channel_id=1, source_target_pairs={{0,15},{1,0},{2,1},{3,2},{4,3},{5,4},{6,5},{7,6},{8,7},{9,8},{10,9... | collective-permute-start | bytes 663560 | tf_op jit(solution)/shard_map/ppermute | solution.py:538
  28.0 15.1 %slice-start.1 = ((s8[8388608]{0:T(1024)(128)(4,1)}), s8[4194304]{0:T(1024)(128)(4,1)S(1)}, s32[]{:S(2)}) async-start(s8[8388608]{0:T(1024)(128)(4,1)} %bitcast.21), calls=%async_computation.2 | async-start | bytes 8388608
  32.3 1.2 copy-start.4
  33.1 10.1 %collective-permute-start.7 = (bf16[224,512]{1,0:T(8,128)(2,1)S(1)}, bf16[224,512]{1,0:T(8,128)(2,1)S(1)}, u32[]{:S(2)}, u32[]{:S(2)}) collective-permute-start(bf16[224,512]{1,0:T(8,128)(2,1)S(1)} %get-tuple-element.82), channel_id=1, source_target_pairs={{0,15},{1,0},{2,1},{3,2},{4,3},{5,4},{6,5},{7,6},{8,7},{9,8},{10,9... | collective-permute-start | bytes 688136 | tf_op jit(solution)/shard_map/ppermute | solution.py:538
  33.5 9.7 %copy-start = (bf16[2048,1024]{1,0:T(8,128)(2,1)S(1)}, bf16[2048,1024]{1,0:T(8,128)(2,1)}, u32[]{:S(2)}) copy-start(bf16[2048,1024]{1,0:T(8,128)(2,1)} %mw_ref.1) | copy-start | bytes 12582916
  33.5 9.7 %copy-start.5 = (f32[2048]{0:T(1024)S(1)}, f32[2048]{0:T(1024)}, u32[]{:S(2)}) copy-start(f32[2048]{0:T(1024)} %param.15) | copy-start | bytes 24580
  33.5 9.7 %copy-start.6 = (f32[1024]{0:T(1024)S(1)}, f32[1024]{0:T(1024)}, u32[]{:S(2)}) copy-start(f32[1024]{0:T(1024)} %param.18) | copy-start | bytes 12292
  33.5 9.7 %copy-start.8 = (f32[16]{0:T(128)S(1)}, f32[16]{0:T(128)}, u32[]{:S(2)}) copy-start(f32[16]{0:T(128)} %scale_ref.1) | copy-start | bytes 196
  33.6 23.8 %collective-permute-start.8 = (bf16[216,512]{1,0:T(8,128)(2,1)S(1)}, bf16[216,512]{1,0:T(8,128)(2,1)S(1)}, u32[]{:S(2)}, u32[]{:S(2)}) collective-permute-start(bf16[216,512]{1,0:T(8,128)(2,1)S(1)} %get-tuple-element.93), channel_id=1, source_target_pairs={{0,15},{1,0},{2,1},{3,2},{4,3},{5,4},{6,5},{7,6},{8,7},{9,8},{10,9... | collective-permute-start | bytes 663560 | tf_op jit(solution)/shard_map/ppermute | solution.py:538
  37.3 20.1 %collective-permute-start.9 = (bf16[162,512]{1,0:T(8,128)(2,1)S(1)}, bf16[162,512]{1,0:T(8,128)(2,1)S(1)}, u32[]{:S(2)}, u32[]{:S(2)}) collective-permute-start(bf16[162,512]{1,0:T(8,128)(2,1)S(1)} %get-tuple-element.94), channel_id=1, source_target_pairs={{0,112},{16,0},{32,16},{48,32},{64,48},{80,64},{96,80},{112,96},{1... | collective-permute-start | bytes 497672 | tf_op jit(solution)/shard_map/ppermute | solution.py:538
  43.0 14.5 %collective-permute-start.10 = (bf16[54,512]{1,0:T(8,128)(2,1)S(1)}, bf16[54,512]{1,0:T(8,128)(2,1)S(1)}, u32[]{:S(2)}, u32[]{:S(2)}) collective-permute-start(bf16[54,512]{1,0:T(8,128)(2,1)S(1)} %get-tuple-element.95), channel_id=1, source_target_pairs={{0,127},{1,112},{2,113},{3,114},{4,115},{5,116},{6,117},{7,118},{8... | collective-permute-start | bytes 165896 | tf_op jit(solution)/shard_map/ppermute | solution.py:548
  57.5 6.0 %collective-permute-start.11 = (bf16[216,512]{1,0:T(8,128)(2,1)S(1)}, bf16[216,512]{1,0:T(8,128)(2,1)S(1)}, u32[]{:S(2)}, u32[]{:S(2)}) collective-permute-start(bf16[216,512]{1,0:T(8,128)(2,1)S(1)} %get-tuple-element.96), channel_id=1, source_target_pairs={{0,1},{1,2},{2,3},{3,4},{4,5},{5,6},{6,7},{7,8},{8,9},{9,10},{10,1... | collective-permute-start | bytes 663560 | tf_op jit(solution)/shard_map/ppermute | solution.py:538
  58.7 17.3 %collective-permute-start.14 = (bf16[162,512]{1,0:T(8,128)(2,1)S(1)}, bf16[162,512]{1,0:T(8,128)(2,1)S(1)}, u32[]{:S(2)}, u32[]{:S(2)}) collective-permute-start(bf16[162,512]{1,0:T(8,128)(2,1)S(1)} %get-tuple-element.113), channel_id=1, source_target_pairs={{0,16},{16,32},{32,48},{48,64},{64,80},{80,96},{96,112},{112,0},{1... | collective-permute-start | bytes 497672 | tf_op jit(solution)/shard_map/ppermute | solution.py:538
  61.7 14.3 %collective-permute-start.15 = (bf16[54,512]{1,0:T(8,128)(2,1)S(1)}, bf16[54,512]{1,0:T(8,128)(2,1)S(1)}, u32[]{:S(2)}, u32[]{:S(2)}) collective-permute-start(bf16[54,512]{1,0:T(8,128)(2,1)S(1)} %get-tuple-element.114), channel_id=1, source_target_pairs={{0,17},{1,18},{2,19},{3,20},{4,21},{5,22},{6,23},{7,24},{8,25},{9,... | collective-permute-start | bytes 165896 | tf_op jit(solution)/shard_map/ppermute | solution.py:548
  63.7 11.1 %collective-permute-start.12 = (bf16[6,3,6,1024]{3,1,0,2:T(4,128)(2,1)S(1)}, bf16[6,3,6,1024]{3,1,0,2:T(4,128)(2,1)S(1)}, u32[]{:S(2)}, u32[]{:S(2)}) collective-permute-start(bf16[6,3,6,1024]{3,1,0,2:T(4,128)(2,1)S(1)} %copy.17), channel_id=1, source_target_pairs={{0,16},{16,32},{32,48},{48,64},{64,80},{80,96},{96,112},{112,0},{1... | collective-permute-start | bytes 663560 | tf_op jit(solution)/shard_map/ppermute | solution.py:538
  82.6 5.6 %collective-permute-start.16 = (bf16[512,1024]{1,0:T(8,128)(2,1)S(1)}, bf16[512,1024]{1,0:T(8,128)(2,1)S(1)}, u32[]{:S(2)}, u32[]{:S(2)}) collective-permute-start(bf16[512,1024]{1,0:T(8,128)(2,1)S(1)} %get-tuple-element.123), channel_id=1, source_target_pairs={{0,1},{1,0},{2,3},{3,2},{4,5},{5,4},{6,7},{7,6},{8,9},{9,8},{10,11... | collective-permute-start | bytes 3145736 | tf_op jit(solution)/shard_map/ppermute | solution.py:616
  88.3 6.2 %copy-start.10 = (bf16[6,3,12,1024]{3,1,0,2:T(4,128)(2,1)S(1)}, bf16[6,3,12,1024]{3,1,0,2:T(4,128)(2,1)}, u32[]{:S(2)}) copy-start(bf16[6,3,12,1024]{3,1,0,2:T(4,128)(2,1)} %pad_maximum_fusion.2) | copy-start | bytes 1327108
  89.7 24.9 %all-to-all-start = ((bf16[64,8,1024]{2,1,0:T(8,128)(2,1)}), bf16[64,8,1024]{2,1,0:T(8,128)(2,1)S(1)}, u32[]{:S(2)}, u32[]{:S(2)}) async-start(bf16[64,8,1024]{2,1,0:T(8,128)(2,1)} %fusion), calls=%async_computation | async-start | bytes 2097152 | tf_op jit(solution)/shard_map/all_to_all | solution.py:563
  95.5 21.9 %collective-permute-start.13 = (bf16[3,3,12,1024]{3,1,0,2:T(4,128)(2,1)}, bf16[3,3,12,1024]{3,1,0,2:T(4,128)(2,1)S(1)}, u32[]{:S(2)}, u32[]{:S(2)}) collective-permute-start(bf16[3,3,12,1024]{3,1,0,2:T(4,128)(2,1)} %get-tuple-element.139), channel_id=1, source_target_pairs={{0,1},{1,2},{2,3},{3,4},{4,5},{5,6},{6,7},{7,8},{8,9},{9,10},{10,1... | collective-permute-start | bytes 663560 | tf_op jit(solution)/shard_map/ppermute | solution.py:538
  97.0 20.4 %collective-permute-start.17 = (bf16[216,512]{1,0:T(8,128)(2,1)S(1)}, bf16[216,512]{1,0:T(8,128)(2,1)S(1)}, u32[]{:S(2)}, u32[]{:S(2)}) collective-permute-start(bf16[216,512]{1,0:T(8,128)(2,1)S(1)} %get-tuple-element.133), channel_id=1, source_target_pairs={{0,1},{1,2},{2,3},{3,4},{4,5},{5,6},{6,7},{7,8},{8,9},{9,10},{10,1... | collective-permute-start | bytes 663560 | tf_op jit(solution)/shard_map/ppermute | solution.py:538
  97.0 21.4 %collective-permute-start.18 = (bf16[162,512]{1,0:T(8,128)(2,1)S(1)}, bf16[162,512]{1,0:T(8,128)(2,1)S(1)}, u32[]{:S(2)}, u32[]{:S(2)}) collective-permute-start(bf16[162,512]{1,0:T(8,128)(2,1)S(1)} %get-tuple-element.135), channel_id=1, source_target_pairs={{0,16},{16,32},{32,48},{48,64},{64,80},{80,96},{96,112},{112,0},{1... | collective-permute-start | bytes 497672 | tf_op jit(solution)/shard_map/ppermute | solution.py:538
  99.7 20.3 %collective-permute-start.19 = (bf16[54,512]{1,0:T(8,128)(2,1)S(1)}, bf16[54,512]{1,0:T(8,128)(2,1)S(1)}, u32[]{:S(2)}, u32[]{:S(2)}) collective-permute-start(bf16[54,512]{1,0:T(8,128)(2,1)S(1)} %get-tuple-element.137), channel_id=1, source_target_pairs={{0,17},{1,18},{2,19},{3,20},{4,21},{5,22},{6,23},{7,24},{8,25},{9,... | collective-permute-start | bytes 165896 | tf_op jit(solution)/shard_map/ppermute | solution.py:548
  114.8 7.8 %collective-permute-start.20 = (f32[4,1024]{1,0:T(4,128)S(1)}, f32[4,1024]{1,0:T(4,128)S(1)}, u32[]{:S(2)}, u32[]{:S(2)}) collective-permute-start(f32[4,1024]{1,0:T(4,128)S(1)} %slice_select_fusion.1), channel_id=1, source_target_pairs={{0,1},{1,0},{2,3},{3,2},{4,5},{5,4},{6,7},{7,6},{8,9},{9,8},{10,11... | collective-permute-start | bytes 49160 | tf_op jit(solution)/shard_map/ppermute | solution.py:571
  120.1 1.3 %copy-start.11 = (bf16[3,3,12,1024]{3,1,0,2:T(4,128)(2,1)S(1)}, bf16[3,3,12,1024]{3,1,0,2:T(4,128)(2,1)}, u32[]{:S(2)}) copy-start(bf16[3,3,12,1024]{3,1,0,2:T(4,128)(2,1)} %get-tuple-element.140) | copy-start | bytes 663556
